TPU v7x, 32 devices: a whole 2x2x4 slice. The times are simulated.
32 devices in a mesh: rows: 8 (over z, y), cols: 4 (over x, core).
Axes of the slice: x: 2, y: 2, z: 4, core: 2. Of those that a mesh axis runs over, the one named last changes fastest.
Arguments:
- pin_features: bfloat16 [8192, 1024], P('rows', 'cols'), may hold values from -6 to 6
- board_features: bfloat16 [8192, 512], P('rows', 'cols'), may hold values from -6 to 6
- is_board: int32 [8192], P('rows'), may hold values 0 or 1
- neighbours: int32 [8192, 50], P('rows'), may hold values from 0 to 8191
- present: int32 [8192, 50], P('rows'), may hold values from 0 to 1, as said below
- importance: float32 [8192, 50], P('rows')
- proj_weight: bfloat16 [512, 1024], P(None, 'cols'), may hold values from -0.25 to 0.25
- proj_bias: float32 [1024], P('cols'), may hold values from -3 to 3
- q_weight: bfloat16 [1024, 1024], P(None, 'cols'), may hold values from -0.1875 to 0.1875
- q_bias: float32 [1024], P('cols'), may hold values from -3 to 3
- w_weight: bfloat16 [2048, 1024], P(None, 'cols'), may hold values from -0.125 to 0.125
- w_bias: float32 [1024], P('cols'), may hold values from -3 to 3
- cotangent: bfloat16 [8192, 1024], P('rows', 'cols'), may hold values from -6 to 6
Outputs:
- embeddings: bfloat16 [8192, 1024], P('rows', 'cols')
- grad_pin: float32 [8192, 1024], P('rows', 'cols')
- grad_board: float32 [8192, 512], P('rows', 'cols')
- grad_proj: float32 [512, 1024], P('rows', 'cols')
- grad_proj_bias: float32 [1024], P('cols')
- grad_q: float32 [1024, 1024], P('rows', 'cols')
- grad_q_bias: float32 [1024], P('cols')
- grad_w: float32 [2048, 1024], P('rows', 'cols')
- grad_w_bias: float32 [1024], P('cols')
- mean_count: float32 [], replicated
- mean_weight: float32 [], replicated
Inputs may be any that keep to these rules, and one draw needn't show every extreme that they name: `present`: each node has 5 to 50 filled slots, some node exactly 5 and some exactly 50.
All inputs are finite; a program needn't handle non-finite values. No bound on the sum of `is_board` on one device may be relied on, other than what follows from the above.
Results may differ from a plain program's by a relative error of at most 0.018.
Values may be sent and summed in bfloat16 or wider, within the bound.
A program may use at most 128 MiB of HBM per device.

v0:
```python
import math

import jax
import jax.numpy as jnp
from jax import lax
from jax.sharding import PartitionSpec as P

SLOTS = 50


def silu_slope(value):
    sig = jax.nn.sigmoid(value)
    return sig * (1.0 + value * (1.0 - sig))


def slot_table(nbr_block, alpha_block, start, width):
    offsets = nbr_block - start
    places = lax.broadcasted_iota(jnp.int32, (1, 1, width), 2)
    return jnp.sum(jnp.where(offsets[:, :, None] == places, alpha_block[:, :, None], 0.0), axis=1)


def split_pair(table):
    upper = table.astype(jnp.bfloat16)
    lower = (table - upper.astype(jnp.float32)).astype(jnp.bfloat16)
    return (upper, lower)


def collect_rows(nbrs, alphas, table_all):
    total, columns = table_all.shape
    col_tile = math.gcd(total, 2048)
    count_tiles = total // col_tile
    tiles = table_all.reshape(count_tiles, col_tile, columns)
    rows = nbrs.shape[0]
    row_block = math.gcd(rows, 512)
    count_rows = rows // row_block

    def one_rows(pair):
        nbr_block, alpha_block = pair

        def step(acc, index):
            upper, lower = split_pair(
                slot_table(nbr_block, alpha_block, index * col_tile, col_tile)
            )
            piece = tiles[index]
            acc = acc + jnp.dot(upper, piece, preferred_element_type=jnp.float32)
            return (acc + jnp.dot(lower, piece, preferred_element_type=jnp.float32), None)

        acc, unused = lax.scan(
            step, jnp.zeros((row_block, columns), jnp.float32), jnp.arange(count_tiles)
        )
        return acc

    out = lax.map(
        one_rows,
        (nbrs.reshape(count_rows, row_block, -1), alphas.reshape(count_rows, row_block, -1)),
    )
    return out.reshape(rows, columns)


def spread_rows(grads, nbrs, alphas, base, width):
    rows, columns = grads.shape
    row_block = math.gcd(rows, 512)
    count_rows = rows // row_block
    col_tile = math.gcd(width, 2048)
    count_tiles = width // col_tile
    stacked = (
        grads.reshape(count_rows, row_block, columns),
        nbrs.reshape(count_rows, row_block, -1),
        alphas.reshape(count_rows, row_block, -1),
    )
    tdot = (((0,), (0,)), ((), ()))

    def one_tile(index):

        def step(acc, triple):
            grad_block, nbr_block, alpha_block = triple
            upper, lower = split_pair(
                slot_table(nbr_block, alpha_block, base + index * col_tile, col_tile)
            )
            acc = acc + lax.dot_general(upper, grad_block, tdot, preferred_element_type=jnp.float32)
            return (
                acc + lax.dot_general(lower, grad_block, tdot, preferred_element_type=jnp.float32),
                None,
            )

        acc, unused = lax.scan(step, jnp.zeros((col_tile, columns), jnp.float32), stacked)
        return acc

    out = lax.map(one_tile, jnp.arange(count_tiles))
    return out.reshape(width, columns)


def per_device(
    pin_features,
    board_features,
    is_board,
    neighbours,
    present,
    importance,
    proj_weight,
    proj_bias,
    q_weight,
    q_bias,
    w_weight,
    w_bias,
    cotangent,
):
    local_rows = pin_features.shape[0]
    width = q_weight.shape[0]
    filled = present.astype(jnp.float32) * importance
    alpha = filled / jnp.sum(filled, axis=1, keepdims=True)
    board_mask = (is_board == 1)[:, None]
    stat_terms = (jnp.sum(present.astype(jnp.float32)), jnp.sum(filled))
    stat_totals = lax.psum((stat_terms[0], stat_terms[1]), "rows")
    board_full = lax.all_gather(board_features, "cols", axis=1, tiled=True)
    board_proj = jnp.dot(board_full, proj_weight, preferred_element_type=jnp.float32) + proj_bias
    h_local = jnp.where(board_mask, board_proj, pin_features.astype(jnp.float32)).astype(
        jnp.bfloat16
    )
    h_full = lax.all_gather(h_local, "cols", axis=1, tiled=True)
    v_pre = jnp.dot(h_full, q_weight, preferred_element_type=jnp.float32) + q_bias
    message = jax.nn.silu(v_pre).astype(jnp.bfloat16)
    message_all = lax.all_gather(message, "rows", axis=0, tiled=True)
    agg_local = collect_rows(neighbours, alpha, message_all).astype(jnp.bfloat16)
    agg_full = lax.all_gather(agg_local, "cols", axis=1, tiled=True)
    w_self = w_weight[:width]
    w_agg = w_weight[width:]
    u_pre = (
        jnp.dot(h_full, w_self, preferred_element_type=jnp.float32)
        + jnp.dot(agg_full, w_agg, preferred_element_type=jnp.float32)
        + w_bias
    )
    z_act = jax.nn.silu(u_pre)
    squares = lax.psum(jnp.sum(z_act * z_act, axis=1), "cols")
    scale = lax.rsqrt(squares + 1e-06)[:, None]
    embeddings = (z_act * scale).astype(jnp.bfloat16)
    grad_out = cotangent.astype(jnp.float32)
    inner = lax.psum(jnp.sum(grad_out * z_act, axis=1), "cols")[:, None]
    grad_z = grad_out * scale - z_act * scale * scale * scale * inner
    grad_u = (grad_z * silu_slope(u_pre)).astype(jnp.bfloat16)
    agg_part = lax.dot_general(
        grad_u, w_agg, (((1,), (1,)), ((), ())), preferred_element_type=jnp.float32
    )
    grad_agg = lax.psum_scatter(agg_part, "cols", scatter_dimension=1, tiled=True).astype(
        jnp.bfloat16
    )
    table = spread_rows(grad_agg, neighbours, alpha, 0, message_all.shape[0])
    grad_message = lax.psum_scatter(
        table.astype(jnp.bfloat16), "rows", scatter_dimension=0, tiled=True
    ).astype(jnp.float32)
    grad_v = (grad_message * silu_slope(v_pre)).astype(jnp.bfloat16)
    h_part = lax.dot_general(
        grad_u, w_self, (((1,), (1,)), ((), ())), preferred_element_type=jnp.float32
    )
    h_part = h_part + lax.dot_general(
        grad_v, q_weight, (((1,), (1,)), ((), ())), preferred_element_type=jnp.float32
    )
    grad_h = lax.psum_scatter(
        h_part.astype(jnp.bfloat16), "cols", scatter_dimension=1, tiled=True
    ).astype(jnp.float32)
    grad_pin = jnp.where(board_mask, 0.0, grad_h)
    grad_hb = jnp.where(board_mask, grad_h, 0.0).astype(jnp.bfloat16)
    board_part = lax.dot_general(
        grad_hb, proj_weight, (((1,), (1,)), ((), ())), preferred_element_type=jnp.float32
    )
    grad_board = lax.psum_scatter(
        board_part.astype(jnp.bfloat16), "cols", scatter_dimension=1, tiled=True
    ).astype(jnp.float32)
    tdot = (((0,), (0,)), ((), ()))
    grad_w_local = jnp.concatenate(
        [
            lax.dot_general(h_full, grad_u, tdot, preferred_element_type=jnp.float32),
            lax.dot_general(agg_full, grad_u, tdot, preferred_element_type=jnp.float32),
        ],
        axis=0,
    )
    grad_q_local = lax.dot_general(h_full, grad_v, tdot, preferred_element_type=jnp.float32)
    grad_p_local = lax.dot_general(board_full, grad_hb, tdot, preferred_element_type=jnp.float32)
    grad_w, grad_q, grad_proj = (
        lax.psum_scatter(
            grad_w_local.astype(jnp.bfloat16), "rows", scatter_dimension=0, tiled=True
        ).astype(jnp.float32),
        lax.psum_scatter(
            grad_q_local.astype(jnp.bfloat16), "rows", scatter_dimension=0, tiled=True
        ).astype(jnp.float32),
        lax.psum_scatter(
            grad_p_local.astype(jnp.bfloat16), "rows", scatter_dimension=0, tiled=True
        ).astype(jnp.float32),
    )
    bias_terms = (
        jnp.sum(grad_hb.astype(jnp.float32), axis=0),
        jnp.sum(grad_v.astype(jnp.float32), axis=0),
        jnp.sum(grad_u.astype(jnp.float32), axis=0),
    )
    grad_pb, grad_qb, grad_wb = lax.psum((bias_terms[0], bias_terms[1], bias_terms[2]), "rows")
    all_nodes = local_rows * lax.axis_size("rows")
    mean_count = stat_totals[0] / all_nodes
    mean_weight = stat_totals[1] / (all_nodes * SLOTS)
    return (
        embeddings,
        grad_pin,
        grad_board,
        grad_proj,
        grad_pb,
        grad_q,
        grad_qb,
        grad_w,
        grad_wb,
        mean_count,
        mean_weight,
    )


def solution(mesh):
    in_specs = (
        P("rows", "cols"),
        P("rows", "cols"),
        P("rows"),
        P("rows", None),
        P("rows", None),
        P("rows", None),
        P(None, "cols"),
        P("cols"),
        P(None, "cols"),
        P("cols"),
        P(None, "cols"),
        P("cols"),
        P("rows", "cols"),
    )
    out_specs = (
        P("rows", "cols"),
        P("rows", "cols"),
        P("rows", "cols"),
        P("rows", "cols"),
        P("cols"),
        P("rows", "cols"),
        P("cols"),
        P("rows", "cols"),
        P("cols"),
        P(),
        P(),
    )
    return jax.shard_map(
        per_device, mesh=mesh, in_specs=in_specs, out_specs=out_specs, check_vma=False
    )
```

profile of v0, /device:TPU:0, one launch (start us, length us, event | category | flops | bytes accessed | tf_op | source)
XLA Modules:
  0.0 1339.8 jit_solution(14868709643257180481)
XLA Ops:
  8.7 20.5 %all-gather.5.cloned.1.call-done = bf16[1024,512]{1,0:T(8,128)(2,1)} async-done(((bf16[1024,128]{1,0:T(8,128)(2,1)}), bf16[1024,512]{1,0:T(8,128)(2,1)}) %all-gather.5.cloned.1.call-update) | async-done | bytes 1048592 | tf_op jit(solution)/shard_map/all_gather | solution.py:115
  31.9 22.9 %all-gather.7.cloned.1.call-done = bf16[1024,1024]{1,0:T(8,128)(2,1)} async-done(((bf16[1024,256]{1,0:T(8,128)(2,1)}), bf16[1024,1024]{1,0:T(8,128)(2,1)}) %all-gather.7.cloned.1.call-update) | async-done | bytes 2097168 | tf_op jit(solution)/shard_map/all_gather | solution.py:120
  54.9 3.6 multiply_convert_fusion.1
  60.4 71.6 %all-gather.9.cloned.1.call-done = bf16[8192,256]{0,1:T(8,128)(2,1)} async-done(((bf16[1024,256]{0,1:T(8,128)(2,1)}), bf16[8192,256]{0,1:T(8,128)(2,1)}) %all-gather.9.cloned.1.call-update) | async-done | bytes 4194320 | tf_op jit(solution)/shard_map/all_gather | solution.py:123
  132.0 6.4 copy.57
  138.4 392.4 %while.45 = (s32[]{:T(128)}, bf16[2,512,256]{2,1,0:T(8,128)(2,1)}, s32[2,512,50]{1,2,0:T(8,128)S(1)}, f32[2,512,50]{1,2,0:T(8,128)}, bf16[4,2048,256]{2,1,0:T(8,...) while((s32[]{:T(128)}, bf16[2,512,256]{2,1,0:T(8,128)(2,1)}, ...), condition=%wide.region_5.6_spmd, body=%wide.region_1.5_spmd.sunk | while | flops 1235641344 | bytes 18645904 | solution.py:53
  139.4 194.5 %while.48 = (s32[]{:T(128)}, f32[512,256]{1,0:T(8,128)S(1)}, s32[4]{0:T(128)S(1)}, s32[512,50]{0,1:T(8,128)S(1)}, f32[512,50]{0,1:T(8,128)S(1)}, /*index=5*/bf16...) while((s32[]{:T(128)}, f32[512,256]{1,0:T(8,128)S(1)}, s32[4]{0:T(128)S(1)}, ...), condition=%wide.region_4.4_spmd.clone, body=%wide.region_2.0_spmd.clone.sunk | while | flops 1235641344 | bytes 17186996 | solution.py:48
  142.6 37.7 %select_reduce_fusion.5 = f32[512,2048]{1,0:T(8,128)} fusion(f32[512,50]{0,1:T(8,128)S(1)} %get-tuple-element.576, s32[512,50]{0,1:T(8,128)S(1)} %broadcast_subtract_fusion.2), kind=kLoop, calls=%fused_computation.clone.1 | loop fusion | flops 156237824 | bytes 4399104 | tf_op jit(solution)/shard_map/while/body/eval_jaxpr/while/body/eval_jaxpr/reduce_sum | solution.py:19
  180.3 4.4 fusion.72
  184.7 3.3 fusion.73
  191.2 37.7 %select_reduce_fusion.5 = f32[512,2048]{1,0:T(8,128)} fusion(f32[512,50]{0,1:T(8,128)S(1)} %get-tuple-element.576, s32[512,50]{0,1:T(8,128)S(1)} %broadcast_subtract_fusion.2), kind=kLoop, calls=%fused_computation.clone.1 | loop fusion | flops 156237824 | bytes 4399104 | tf_op jit(solution)/shard_map/while/body/eval_jaxpr/while/body/eval_jaxpr/reduce_sum | solution.py:19
  228.9 4.4 fusion.72
  233.3 3.3 fusion.73
  239.9 37.7 %select_reduce_fusion.5 = f32[512,2048]{1,0:T(8,128)} fusion(f32[512,50]{0,1:T(8,128)S(1)} %get-tuple-element.576, s32[512,50]{0,1:T(8,128)S(1)} %broadcast_subtract_fusion.2), kind=kLoop, calls=%fused_computation.clone.1 | loop fusion | flops 156237824 | bytes 4399104 | tf_op jit(solution)/shard_map/while/body/eval_jaxpr/while/body/eval_jaxpr/reduce_sum | solution.py:19
  277.5 4.4 fusion.72
  281.9 3.3 fusion.73
  288.5 37.7 %select_reduce_fusion.5 = f32[512,2048]{1,0:T(8,128)} fusion(f32[512,50]{0,1:T(8,128)S(1)} %get-tuple-element.576, s32[512,50]{0,1:T(8,128)S(1)} %broadcast_subtract_fusion.2), kind=kLoop, calls=%fused_computation.clone.1 | loop fusion | flops 156237824 | bytes 4399104 | tf_op jit(solution)/shard_map/while/body/eval_jaxpr/while/body/eval_jaxpr/reduce_sum | solution.py:19
  326.1 4.4 fusion.72
  330.6 3.3 fusion.73
  335.6 194.5 %while.48 = (s32[]{:T(128)}, f32[512,256]{1,0:T(8,128)S(1)}, s32[4]{0:T(128)S(1)}, s32[512,50]{0,1:T(8,128)S(1)}, f32[512,50]{0,1:T(8,128)S(1)}, /*index=5*/bf16...) while((s32[]{:T(128)}, f32[512,256]{1,0:T(8,128)S(1)}, s32[4]{0:T(128)S(1)}, ...), condition=%wide.region_4.4_spmd.clone, body=%wide.region_2.0_spmd.clone.sunk | while | flops 1235641344 | bytes 17186996 | solution.py:48
  338.8 37.7 %select_reduce_fusion.5 = f32[512,2048]{1,0:T(8,128)} fusion(f32[512,50]{0,1:T(8,128)S(1)} %get-tuple-element.576, s32[512,50]{0,1:T(8,128)S(1)} %broadcast_subtract_fusion.2), kind=kLoop, calls=%fused_computation.clone.1 | loop fusion | flops 156237824 | bytes 4399104 | tf_op jit(solution)/shard_map/while/body/eval_jaxpr/while/body/eval_jaxpr/reduce_sum | solution.py:19
  376.4 4.4 fusion.72
  380.8 3.3 fusion.73
  387.4 37.7 %select_reduce_fusion.5 = f32[512,2048]{1,0:T(8,128)} fusion(f32[512,50]{0,1:T(8,128)S(1)} %get-tuple-element.576, s32[512,50]{0,1:T(8,128)S(1)} %broadcast_subtract_fusion.2), kind=kLoop, calls=%fused_computation.clone.1 | loop fusion | flops 156237824 | bytes 4399104 | tf_op jit(solution)/shard_map/while/body/eval_jaxpr/while/body/eval_jaxpr/reduce_sum | solution.py:19
  425.0 4.4 fusion.72
  429.5 3.3 fusion.73
  436.0 37.7 %select_reduce_fusion.5 = f32[512,2048]{1,0:T(8,128)} fusion(f32[512,50]{0,1:T(8,128)S(1)} %get-tuple-element.576, s32[512,50]{0,1:T(8,128)S(1)} %broadcast_subtract_fusion.2), kind=kLoop, calls=%fused_computation.clone.1 | loop fusion | flops 156237824 | bytes 4399104 | tf_op jit(solution)/shard_map/while/body/eval_jaxpr/while/body/eval_jaxpr/reduce_sum | solution.py:19
  473.7 4.4 fusion.72
  478.1 3.3 fusion.73
  484.6 37.7 %select_reduce_fusion.5 = f32[512,2048]{1,0:T(8,128)} fusion(f32[512,50]{0,1:T(8,128)S(1)} %get-tuple-element.576, s32[512,50]{0,1:T(8,128)S(1)} %broadcast_subtract_fusion.2), kind=kLoop, calls=%fused_computation.clone.1 | loop fusion | flops 156237824 | bytes 4399104 | tf_op jit(solution)/shard_map/while/body/eval_jaxpr/while/body/eval_jaxpr/reduce_sum | solution.py:19
  522.3 4.4 fusion.72
  526.7 3.3 fusion.73
  532.1 3.3 fusion.33
  535.5 16.6 %all-gather.11.cloned.1.call-done = bf16[1024,1024]{1,0:T(8,128)(2,1)} async-done(((bf16[1024,256]{1,0:T(8,128)(2,1)}), bf16[1024,1024]{1,0:T(8,128)(2,1)}) %all-gather.11.cloned.1.call-update) | async-done | bytes 2097168 | tf_op jit(solution)/shard_map/all_gather | solution.py:125
  552.1 3.9 fusion.25
  555.9 6.0 all-reduce.1
  562.0 3.3 convert_reduce_fusion
  569.1 45.5 %reduce-scatter.12.cloned.1.call-done = f32[1024,256]{1,0:T(8,128)} async-done(((f32[1024,1024]{1,0:T(8,128)}), f32[1024,256]{1,0:T(8,128)}) %reduce-scatter.12.cloned.1.call-update) | async-done | bytes 1048592 | tf_op jit(solution)/shard_map/reduce_scatter | solution.py:144
  615.9 358.6 %while.47 = (s32[]{:T(128)}, bf16[4,2048,256]{2,1,0:T(8,128)(2,1)}, s32[4]{0:T(128)S(1)}, s32[2,512,50]{1,2,0:T(8,128)S(1)}, f32[2,512,50]{1,2,0:T(8,128)}, /*in...) while((s32[]{:T(128)}, bf16[4,2048,256]{2,1,0:T(8,128)(2,1)}, ...), condition=%wide.region_15.16_spmd, body=%wide.region_11.15_spmd.sunk | while | flops 1236820992 | bytes 44721044 | solution.py:89
  617.1 87.3 %while.49 = (s32[]{:T(128)}, f32[2048,256]{1,0:T(8,128)S(1)}, s32[2,512,50]{1,2,0:T(8,128)S(1)}, s32[]{:T(128)}, f32[2,512,50]{1,2,0:T(8,128)}, /*index=5*/bf16[2,512,256]{2,1,0:T(8,128)(2,1)S(1)}, s32[]{:T(128)}, s32[]{:T(128)}) while((s32[]{:T(128)}, f32[2048,256]{1,0:T(8,128)S(1)}, s32[2,512,50]{1,2,0:T(8,128)S(1)}, ...), condition=%wide.region_14.14_spmd.clone, body=%wide.region_12.13_spmd.clone.sunk | while | flops 1236820992 | bytes 40526024 | solution.py:86
  618.7 37.7 %select_reduce_fusion.4 = f32[512,2048]{1,0:T(8,128)} fusion(f32[512,50]{0,1:T(8,128)S(1)} %dynamic-slice_bitcast_fusion.8, s32[512,50]{0,1:T(8,128)S(1)} %subtract_bitcast_fusion.2), kind=kLoop, calls=%fused_computation.18.clone.1 | loop fusion | flops 156237824 | bytes 4399104 | tf_op jit(solution)/shard_map/while/body/eval_jaxpr/while/body/eval_jaxpr/reduce_sum | solution.py:19
  656.4 3.1 convolution_add_fusion.8
  662.4 37.7 %select_reduce_fusion.4 = f32[512,2048]{1,0:T(8,128)} fusion(f32[512,50]{0,1:T(8,128)S(1)} %dynamic-slice_bitcast_fusion.8, s32[512,50]{0,1:T(8,128)S(1)} %subtract_bitcast_fusion.2), kind=kLoop, calls=%fused_computation.18.clone.1 | loop fusion | flops 156237824 | bytes 4399104 | tf_op jit(solution)/shard_map/while/body/eval_jaxpr/while/body/eval_jaxpr/reduce_sum | solution.py:19
  706.7 87.3 %while.49 = (s32[]{:T(128)}, f32[2048,256]{1,0:T(8,128)S(1)}, s32[2,512,50]{1,2,0:T(8,128)S(1)}, s32[]{:T(128)}, f32[2,512,50]{1,2,0:T(8,128)}, /*index=5*/bf16[2,512,256]{2,1,0:T(8,128)(2,1)S(1)}, s32[]{:T(128)}, s32[]{:T(128)}) while((s32[]{:T(128)}, f32[2048,256]{1,0:T(8,128)S(1)}, s32[2,512,50]{1,2,0:T(8,128)S(1)}, ...), condition=%wide.region_14.14_spmd.clone, body=%wide.region_12.13_spmd.clone.sunk | while | flops 1236820992 | bytes 40526024 | solution.py:86
  708.3 37.7 %select_reduce_fusion.4 = f32[512,2048]{1,0:T(8,128)} fusion(f32[512,50]{0,1:T(8,128)S(1)} %dynamic-slice_bitcast_fusion.8, s32[512,50]{0,1:T(8,128)S(1)} %subtract_bitcast_fusion.2), kind=kLoop, calls=%fused_computation.18.clone.1 | loop fusion | flops 156237824 | bytes 4399104 | tf_op jit(solution)/shard_map/while/body/eval_jaxpr/while/body/eval_jaxpr/reduce_sum | solution.py:19
  752.0 37.7 %select_reduce_fusion.4 = f32[512,2048]{1,0:T(8,128)} fusion(f32[512,50]{0,1:T(8,128)S(1)} %dynamic-slice_bitcast_fusion.8, s32[512,50]{0,1:T(8,128)S(1)} %subtract_bitcast_fusion.2), kind=kLoop, calls=%fused_computation.18.clone.1 | loop fusion | flops 156237824 | bytes 4399104 | tf_op jit(solution)/shard_map/while/body/eval_jaxpr/while/body/eval_jaxpr/reduce_sum | solution.py:19
  789.6 3.1 convolution_add_fusion.8
  796.4 87.3 %while.49 = (s32[]{:T(128)}, f32[2048,256]{1,0:T(8,128)S(1)}, s32[2,512,50]{1,2,0:T(8,128)S(1)}, s32[]{:T(128)}, f32[2,512,50]{1,2,0:T(8,128)}, /*index=5*/bf16[2,512,256]{2,1,0:T(8,128)(2,1)S(1)}, s32[]{:T(128)}, s32[]{:T(128)}) while((s32[]{:T(128)}, f32[2048,256]{1,0:T(8,128)S(1)}, s32[2,512,50]{1,2,0:T(8,128)S(1)}, ...), condition=%wide.region_14.14_spmd.clone, body=%wide.region_12.13_spmd.clone.sunk | while | flops 1236820992 | bytes 40526024 | solution.py:86
  798.0 37.7 %select_reduce_fusion.4 = f32[512,2048]{1,0:T(8,128)} fusion(f32[512,50]{0,1:T(8,128)S(1)} %dynamic-slice_bitcast_fusion.8, s32[512,50]{0,1:T(8,128)S(1)} %subtract_bitcast_fusion.2), kind=kLoop, calls=%fused_computation.18.clone.1 | loop fusion | flops 156237824 | bytes 4399104 | tf_op jit(solution)/shard_map/while/body/eval_jaxpr/while/body/eval_jaxpr/reduce_sum | solution.py:19
  835.7 3.1 convolution_add_fusion.8
  841.7 37.7 %select_reduce_fusion.4 = f32[512,2048]{1,0:T(8,128)} fusion(f32[512,50]{0,1:T(8,128)S(1)} %dynamic-slice_bitcast_fusion.8, s32[512,50]{0,1:T(8,128)S(1)} %subtract_bitcast_fusion.2), kind=kLoop, calls=%fused_computation.18.clone.1 | loop fusion | flops 156237824 | bytes 4399104 | tf_op jit(solution)/shard_map/while/body/eval_jaxpr/while/body/eval_jaxpr/reduce_sum | solution.py:19
  886.0 87.3 %while.49 = (s32[]{:T(128)}, f32[2048,256]{1,0:T(8,128)S(1)}, s32[2,512,50]{1,2,0:T(8,128)S(1)}, s32[]{:T(128)}, f32[2,512,50]{1,2,0:T(8,128)}, /*index=5*/bf16[2,512,256]{2,1,0:T(8,128)(2,1)S(1)}, s32[]{:T(128)}, s32[]{:T(128)}) while((s32[]{:T(128)}, f32[2048,256]{1,0:T(8,128)S(1)}, s32[2,512,50]{1,2,0:T(8,128)S(1)}, ...), condition=%wide.region_14.14_spmd.clone, body=%wide.region_12.13_spmd.clone.sunk | while | flops 1236820992 | bytes 40526024 | solution.py:86
  887.6 37.7 %select_reduce_fusion.4 = f32[512,2048]{1,0:T(8,128)} fusion(f32[512,50]{0,1:T(8,128)S(1)} %dynamic-slice_bitcast_fusion.8, s32[512,50]{0,1:T(8,128)S(1)} %subtract_bitcast_fusion.2), kind=kLoop, calls=%fused_computation.18.clone.1 | loop fusion | flops 156237824 | bytes 4399104 | tf_op jit(solution)/shard_map/while/body/eval_jaxpr/while/body/eval_jaxpr/reduce_sum | solution.py:19
  931.3 37.7 %select_reduce_fusion.4 = f32[512,2048]{1,0:T(8,128)} fusion(f32[512,50]{0,1:T(8,128)S(1)} %dynamic-slice_bitcast_fusion.8, s32[512,50]{0,1:T(8,128)S(1)} %subtract_bitcast_fusion.2), kind=kLoop, calls=%fused_computation.18.clone.1 | loop fusion | flops 156237824 | bytes 4399104 | tf_op jit(solution)/shard_map/while/body/eval_jaxpr/while/body/eval_jaxpr/reduce_sum | solution.py:19
  974.4 6.3 copy.58
  984.9 84.4 %reduce-scatter.14.cloned.1.call-done = bf16[1024,256]{0,1:T(8,128)(2,1)} async-done(((bf16[8192,256]{0,1:T(8,128)(2,1)}), bf16[1024,256]{0,1:T(8,128)(2,1)}) %reduce-scatter.14.cloned.1.call-update) | async-done | bytes 524304 | tf_op jit(solution)/shard_map/reduce_scatter | solution.py:148
  1070.8 4.3 add_convert_fusion
  1079.6 3.5 convolution_convert_fusion.3
  1083.1 23.3 %reduce-scatter.16.cloned.1.call-done = bf16[1024,256]{1,0:T(8,128)(2,1)} async-done(((bf16[1024,1024]{1,0:T(8,128)(2,1)}), bf16[1024,256]{1,0:T(8,128)(2,1)}) %reduce-scatter.16.cloned.1.call-update) | async-done | bytes 524304 | tf_op jit(solution)/shard_map/reduce_scatter | solution.py:158
  1112.4 61.8 %reduce-scatter.20.cloned.1.call-done = bf16[256,256]{1,0:T(8,128)(2,1)} async-done(((bf16[2048,256]{1,0:T(8,128)(2,1)}), bf16[256,256]{1,0:T(8,128)(2,1)}) %reduce-scatter.20.cloned.1.call-update) | async-done | bytes 131088 | tf_op jit(solution)/shard_map/reduce_scatter | solution.py:180
  1175.9 62.7 %reduce-scatter.18.cloned.1.call-done = bf16[128,256]{1,0:T(8,128)(2,1)} async-done(((bf16[1024,256]{1,0:T(8,128)(2,1)}), bf16[128,256]{1,0:T(8,128)(2,1)}) %reduce-scatter.18.cloned.1.call-update) | async-done | bytes 65552 | tf_op jit(solution)/shard_map/reduce_scatter | solution.py:183
  1241.4 20.2 %all-reduce = (f32[256]{0:T(256)}, f32[256]{0:T(256)}, f32[256]{0:T(256)}, f32[]{:T(128)}, f32[]{:T(128)}) all-reduce(f32[256]{0:T(256)S(1)} %get-tuple-element.351, f32[256]{0:T(256)S(1)} %get-tuple-element.348, f32[256]{0:T(256)S(1)} %copy-done.18, f32[]{:T(128)} %get-tuple-element.292, ...), channel_id=1, replica_groups=mesh['rows'=8,'cols'=4] {'rows'}, use_global_device_ids=true, to_apply=%region_21.22 | all-reduce | flops 770 | bytes 6160 | tf_op jit(solution)/shard_map/psum | solution.py:195
  1262.8 39.6 %reduce-scatter.24.cloned.1.call-done = bf16[64,256]{1,0:T(8,128)(2,1)} async-done(((bf16[512,256]{1,0:T(8,128)(2,1)}), bf16[64,256]{1,0:T(8,128)(2,1)}) %reduce-scatter.24.cloned.1.call-update) | async-done | bytes 32784
  1304.0 25.0 %reduce-scatter.22.cloned.1.call-done = bf16[128,1024]{1,0:T(8,128)(2,1)} async-done(((bf16[512,1024]{1,0:T(8,128)(2,1)}), bf16[128,1024]{1,0:T(8,128)(2,1)}) %reduce-scatter.22.cloned.1.call-update) | async-done | bytes 262160
  (205 shorter events, 89.7 us)
Async XLA Ops:
  7.2 47.7 %copy-start = (bf16[1024,256]{1,0:T(8,128)(2,1)S(1)}, bf16[1024,256]{1,0:T(8,128)(2,1)}, u32[]{:S(2)}) copy-start(bf16[1024,256]{1,0:T(8,128)(2,1)} %param.29) | copy-start | bytes 1572868
  7.2 47.7 %copy-start.19 = (f32[256]{0:T(256)S(1)}, f32[256]{0:T(256)}, u32[]{:S(2)}) copy-start(f32[256]{0:T(256)} %param.30) | copy-start | bytes 3076
  7.2 22.0 %all-gather.5.cloned.1.call-start = ((), (), s32[]{:S(2)}) async-start(), calls=%async_computation.7 | async-start | bytes 1310720 | tf_op jit(solution)/shard_map/all_gather | solution.py:115
  7.9 46.9 %all-gather.7.cloned.1.call-start = ((), (), s32[]{:S(2)}) async-start(), calls=%async_computation.8 | async-start | bytes 2621440 | tf_op jit(solution)/shard_map/all_gather | solution.py:120
  8.7 23.2 %copy-start.16 = (pred[1024]{0:T(1024)(128)(4,1)}, pred[1024]{0:T(1024)(128)(4,1)S(1)}, u32[]{:S(2)}) copy-start(pred[1024]{0:T(1024)(128)(4,1)S(1)} %broadcast_compare_fusion) | copy-start | bytes 3076
  31.9 26.6 %copy-start.12 = (f32[1024,50]{0,1:T(8,128)S(1)}, f32[1024,50]{0,1:T(8,128)}, u32[]{:S(2)}) copy-start(f32[1024,50]{0,1:T(8,128)} %param.26) | copy-start | bytes 614404
  31.9 26.6 %copy-start.13 = (s32[1024,50]{0,1:T(8,128)S(1)}, s32[1024,50]{0,1:T(8,128)}, u32[]{:S(2)}) copy-start(s32[1024,50]{0,1:T(8,128)} %param.25) | copy-start | bytes 614404
  31.9 100.1 %all-gather.9.cloned.1.call-start = ((), (), s32[]{:S(2)}) async-start(), calls=%async_computation.9 | async-start | bytes 4718592 | tf_op jit(solution)/shard_map/all_gather | solution.py:123
  58.4 1.7 copy-start.15
  58.5 493.6 %all-gather.11.cloned.1.call-start = ((), (), s32[]{:S(2)}) async-start(), calls=%async_computation.10 | async-start | bytes 2621440 | tf_op jit(solution)/shard_map/all_gather | solution.py:125
  138.4 393.8 %copy-start.6 = (bf16[2048,256]{1,0:T(8,128)(2,1)S(1)}, bf16[2048,256]{1,0:T(8,128)(2,1)}, u32[]{:S(2)}) copy-start(bf16[2048,256]{1,0:T(8,128)(2,1)} %param.31) | copy-start | bytes 3145732
  530.8 21.3 %copy-start.20 = (f32[256]{0:T(256)S(1)}, f32[256]{0:T(256)}, u32[]{:S(2)}) copy-start(f32[256]{0:T(256)} %param.32) | copy-start | bytes 3076
  530.8 83.7 %reduce-scatter.12.cloned.1.call-start = ((), (), s32[]{:S(2)}) async-start(), calls=%async_computation.11 | async-start | bytes 5242880 | tf_op jit(solution)/shard_map/reduce_scatter | solution.py:144
  565.3 0.8 copy-start.4
  568.8 500.4 %reduce-scatter.14.cloned.1.call-start = ((), (), s32[]{:S(2)}) async-start(), calls=%async_computation.12 | async-start | bytes 4718592 | tf_op jit(solution)/shard_map/reduce_scatter | solution.py:148
  617.1 0.7 copy-start.2
  656.4 3.4 copy-start.1
  659.8 0.9 copy-start.3
  660.8 0.7 copy-start.2
  700.0 3.4 copy-start.1
  703.5 0.9 copy-start.3
  706.7 0.7 copy-start.2
  746.0 3.4 copy-start.1
  749.4 0.9 copy-start.3
  750.4 0.7 copy-start.2
  789.6 3.4 copy-start.1
  793.1 0.9 copy-start.3
  796.4 0.7 copy-start.2
  835.7 3.4 copy-start.1
  839.1 0.9 copy-start.3
  840.1 0.7 copy-start.2
  879.3 3.4 copy-start.1
  882.8 0.9 copy-start.3
  886.0 0.7 copy-start.2
  925.3 3.4 copy-start.1
  928.7 0.9 copy-start.3
  929.7 0.7 copy-start.2
  968.9 3.4 copy-start.1
  972.4 0.9 copy-start.3
  980.8 1.0 copy-start.5
  980.8 1.4 copy-start.7
  980.8 88.5 %copy-start.11 = (f32[1024,256]{0,1:T(8,128)S(1)}, f32[1024,256]{0,1:T(8,128)}, u32[]{:S(2)}) copy-start(f32[1024,256]{0,1:T(8,128)} %get-tuple-element.354) | copy-start | bytes 3145732
  980.8 125.6 %reduce-scatter.16.cloned.1.call-start = ((), (), s32[]{:S(2)}) async-start(), calls=%async_computation.13 | async-start | bytes 2621440 | tf_op jit(solution)/shard_map/reduce_scatter | solution.py:158
  1075.1 99.2 %reduce-scatter.20.cloned.1.call-start = ((), (), s32[]{:S(2)}) async-start(), calls=%async_computation.15 | async-start | bytes 1179648 | tf_op jit(solution)/shard_map/reduce_scatter | solution.py:180
  1075.1 2.5 copy-start.8
  1079.5 26.9 %copy-start.17 = (pred[1024]{0:T(1024)(128)(4,1)S(1)}, pred[1024]{0:T(1024)(128)(4,1)}, u32[]{:S(2)}) copy-start(pred[1024]{0:T(1024)(128)(4,1)} %copy-done.16) | copy-start | bytes 3076
  1079.5 159.1 %reduce-scatter.18.cloned.1.call-start = ((), (), s32[]{:S(2)}) async-start(), calls=%async_computation.14 | async-start | bytes 589824 | tf_op jit(solution)/shard_map/reduce_scatter | solution.py:183
  1083.0 26.6 %copy-start.14 = (bf16[512,256]{1,0:T(8,128)(2,1)S(1)}, bf16[512,256]{1,0:T(8,128)(2,1)}, u32[]{:S(2)}) copy-start(bf16[512,256]{1,0:T(8,128)(2,1)} %param.27) | copy-start | bytes 786436
  1083.1 219.4 %reduce-scatter.24.cloned.1.call-start = ((), (), s32[]{:S(2)}) async-start(), calls=%async_computation.17 | async-start | bytes 294912
  1106.5 3.2 copy-start.10
  1109.5 1.9 copy-start.9
  1109.6 219.5 %reduce-scatter.22.cloned.1.call-start = ((), (), s32[]{:S(2)}) async-start(), calls=%async_computation.16 | async-start | bytes 1310720
  1111.4 129.9 %copy-start.18 = (f32[256]{0:T(256)S(1)}, f32[256]{0:T(256)}, u32[]{:S(2)}) copy-start(f32[256]{0:T(256)} %get-tuple-element.346) | copy-start | bytes 3076
Sparse Core Ops, SparseCore 0:
  9.6 19.5 all-gather.4
  32.0 22.8 all-gather.6
  58.6 73.3 all-gather.8
  530.9 21.0 all-gather.10
  569.0 45.5 reduce-scatter.11
  980.9 88.2 reduce-scatter.13
  1075.2 31.1 reduce-scatter.15
  1110.8 63.3 reduce-scatter.19
  1177.6 60.9 reduce-scatter.17
  1242.1 60.2 reduce-scatter.23
  1305.1 23.9 reduce-scatter.21
where the time goes:
time: 1340 us
  other arithmetic  617 us (46%)
  waiting for transfers between devices  475 us (35%)
  matrix products  125 us (9%)
  local copies, waits for them, and re-layouts  54.7 us (4%)
  blocking collectives  26.2 us (2%)
  loops' own time  24.1 us (2%)
  between operations  17.7 us (1%)
    reduce_sum x16, other arithmetic, slot_table(): jnp.sum(jnp.where(offsets[:, :, None] == places, alpha_block[:, :, None],...  603 us
    reduce_scatter x1, waiting for transfers between devices, per_device(): lax.psum_scatter(table.astype(jnp.bfloat16), 'rows', scatter_dimension=0,...  84.4 us
    all_gather x1, waiting for transfers between devices, per_device(): message_all = lax.all_gather(message, 'rows', axis=0, tiled=True)  71.6 us
    unnamed x13, waiting for transfers between devices  65.5 us
    reduce_scatter x1, waiting for transfers between devices, per_device(): lax.psum_scatter(grad_q_local.astype(jnp.bfloat16), 'rows', scatter_dimen...  62.7 us
    reduce_scatter x1, waiting for transfers between devices, per_device(): lax.psum_scatter(grad_w_local.astype(jnp.bfloat16), 'rows', scatter_dimen...  61.8 us
    reduce_scatter x1, waiting for transfers between devices, per_device(): lax.psum_scatter(agg_part, 'cols', scatter_dimension=1, tiled=True)  45.5 us
    dot_general x8, matrix products, step(): jnp.dot(lower, piece, preferred_element_type=jnp.float32)  35.3 us
  transfers between devices with their start and end apart: 11, of which 11 were waited for; matrix products, arithmetic and copies ran while one was open for 2% of the time, Pallas kernels for 0%

commit v1 on v0

--- a/solution.py
+++ b/solution.py
@@ -1,11 +1,826 @@
+import functools
 import math
 
 import jax
 import jax.numpy as jnp
 from jax import lax
+from jax.experimental import pallas as pl
+from jax.experimental.pallas import tpu as pltpu
 from jax.sharding import PartitionSpec as P
 
 SLOTS = 50
+MESH = pl.DeviceIdType.MESH
+BF = jnp.bfloat16
+F32 = jnp.float32
+NQ = 4
+LO = 128
+PIECE = 64
+NT = (((1,), (1,)), ((), ()))
+TN = (((0,), (0,)), ((), ()))
+
+
+def dot(a, b):
+    return jnp.dot(a, b, preferred_element_type=F32)
+
+
+def dot_nt(a, b):
+    return lax.dot_general(a, b, NT, preferred_element_type=F32)
+
+
+def dot_tn(a, b):
+    return lax.dot_general(a, b, TN, preferred_element_type=F32)
+
+
+def loop(n, body, unroll=1):
+    def step(i, carry):
+        body(i)
+        return carry
+
+    lax.fori_loop(0, n, step, 0, unroll=unroll)
+
+
+def row_sums(x):
+    y = x[:, :128] + x[:, 128:]
+    return jnp.concatenate(
+        [jnp.sum(y[i * 128 : (i + 1) * 128].T, axis=0, keepdims=True) for i in range(2)], axis=0
+    )
+
+
+def down(row):
+    return jnp.broadcast_to(row, (128, 128)).T
+
+
+def down_pair(rows):
+    col = jnp.concatenate([down(rows[0:1]), down(rows[1:2])], axis=0)
+    return jnp.concatenate([col, col], axis=1)
+
+
+def fused_kernel(*refs, names):
+    s = dict(zip(names, refs))
+    r = lax.axis_index("rows")
+    c = lax.axis_index("cols")
+    z, y = r // 2, r % 2
+    x, k = c // 2, c % 2
+    rows, width = s["pin"].shape
+    bwidth = s["board"].shape[1]
+    chunk = rows // NQ
+    zn = 4
+    core = (r, x * 2 + 1 - k)
+    xp = (r, (1 - x) * 2 + k)
+    xk = (r, (1 - x) * 2 + 1 - k)
+    yp = (z * 2 + 1 - y, c)
+
+    def at(q):
+        return pl.ds(pl.multiple_of(q * chunk, chunk), chunk)
+
+    def rdma(src, dst, send, recv, dev):
+        return pltpu.make_async_remote_copy(
+            src_ref=src, dst_ref=dst, send_sem=send, recv_sem=recv, device_id=dev, device_id_type=MESH
+        )
+
+    def arrived(ref, sem):
+        rdma(ref, ref, sem, sem, core).wait_recv()
+
+    def sent(ref, sem):
+        rdma(ref, ref, sem, sem, core).wait_send()
+
+    class Gather:
+        def __init__(self, buf, base, ss, rs):
+            self.buf, self.base, self.ss, self.rs = buf, base, ss, rs
+
+        def ref(self, col, q):
+            return self.buf.at[self.base + col, at(q)]
+
+        def start(self, q):
+            own = self.ref(c, q)
+            rdma(own, own, self.ss.at[1, q], self.rs.at[1, q], xp).start()
+            rdma(own, own, self.ss.at[0, q], self.rs.at[0, q], core).start()
+
+        def forward(self, q):
+            got = self.ref((1 - x) * 2 + k, q)
+            arrived(got, self.rs.at[1, q])
+            rdma(got, got, self.ss.at[2, q], self.rs.at[2, q], core).start()
+
+        def finish(self, q):
+            arrived(self.ref(x * 2 + 1 - k, q), self.rs.at[0, q])
+            arrived(self.ref((1 - x) * 2 + 1 - k, q), self.rs.at[2, q])
+
+        def drain(self, q):
+            for i in range(3):
+                sent(self.ref(c, q), self.ss.at[i, q])
+
+    class Scatter:
+        def __init__(self, part, name):
+            self.part = part
+            self.send1, self.recv1 = s[name + "_send1"], s[name + "_recv1"]
+            self.sendx, self.recvx = s[name + "_sendx"], s[name + "_recvx"]
+            self.ss, self.rs = s[name + "_ss"], s[name + "_rs"]
+
+        def first(self, q):
+            for i, xs in ((0, 1 - x), (1, x)):
+                self.send1[i, q] = self.part(xs * 2 + 1 - k, q).astype(BF)
+                rdma(
+                    self.send1.at[i, q], self.recv1.at[i, q], self.ss.at[i, q], self.rs.at[i, q], core
+                ).start()
+
+        def second(self, q):
+            own = self.part((1 - x) * 2 + k, q)
+            arrived(self.recv1.at[0, q], self.rs.at[0, q])
+            self.sendx[q] = (own + self.recv1[0, q].astype(F32)).astype(BF)
+            rdma(self.sendx.at[q], self.recvx.at[q], self.ss.at[2, q], self.rs.at[2, q], xp).start()
+
+        def third(self, q):
+            own = self.part(c, q)
+            arrived(self.recv1.at[1, q], self.rs.at[1, q])
+            own = own + self.recv1[1, q].astype(F32)
+            arrived(self.recvx.at[q], self.rs.at[2, q])
+            return own + self.recvx[q].astype(F32)
+
+        def drain(self, q):
+            for i in range(2):
+                sent(self.send1.at[i, q], self.ss.at[i, q])
+            sent(self.sendx.at[q], self.ss.at[2, q])
+
+    class WeightSum:
+        def __init__(self, part, name, out):
+            self.part, self.out = part, out
+            self.ysend, self.yrecv = s[name + "_ysend"], s[name + "_yrecv"]
+            self.zsend, self.zrecv = s[name + "_zsend"], s[name + "_zrecv"]
+            self.ss, self.rs = s[name + "_ss"], s[name + "_rs"]
+
+        def first(self):
+            def step(d):
+                self.ysend[d] = self.part(d, 1 - y).astype(BF)
+                rdma(self.ysend.at[d], self.yrecv.at[d], self.ss.at[0, d], self.rs.at[0, d], yp).start()
+
+            loop(zn, step)
+
+        def second(self):
+            def step(d):
+                own = self.part(d, y)
+                arrived(self.yrecv.at[d], self.rs.at[0, d])
+                own = own + self.yrecv[d].astype(F32)
+
+                @pl.when(d == z)
+                def _():
+                    self.out[...] = own
+
+                @pl.when(d != z)
+                def _():
+                    self.zsend[d] = own.astype(BF)
+                    rdma(
+                        self.zsend.at[d],
+                        self.zrecv.at[z],
+                        self.ss.at[1, d],
+                        self.rs.at[1, z],
+                        (d * 2 + y, c),
+                    ).start()
+
+            loop(zn, step)
+
+        def third(self):
+            def step(d):
+                @pl.when(d != z)
+                def _():
+                    arrived(self.zrecv.at[d], self.rs.at[1, d])
+                    self.out[...] += self.zrecv[d].astype(F32)
+
+            loop(zn, step)
+
+        def drain(self):
+            def step(d):
+                sent(self.ysend.at[d], self.ss.at[0, d])
+
+                @pl.when(d != z)
+                def _():
+                    sent(self.zsend.at[d], self.ss.at[1, d])
+
+            loop(zn, step)
+
+    barrier = pltpu.get_barrier_semaphore()
+    greeted = [(r, (c + d) % 4) for d in range(1, 4)] + [((r + d) % 8, c) for d in range(1, 8)]
+    for dev in greeted:
+        pl.semaphore_signal(barrier, inc=1, device_id=dev, device_id_type=MESH)
+
+    boards, own_h = s["boards"], s["ha"]
+    boards[c] = s["board"][...]
+
+    filled = s["present"][...].astype(F32) * s["importance"][...]
+    alpha = filled / jnp.sum(filled, axis=1, keepdims=True)
+    half = rows // 2
+    gap = 64 - SLOTS
+
+    def pairs(a):
+        pad = jnp.zeros((half, gap), a.dtype)
+        return jnp.concatenate([a[:half], pad, a[half:], pad], axis=1)
+
+    small = s["small"]
+    small[...] = jnp.zeros_like(small)
+    sums = jnp.concatenate(
+        [
+            jnp.broadcast_to(jnp.sum(s["present"][...].astype(F32)).reshape(1, 1), (1, 128)),
+            jnp.broadcast_to(jnp.sum(filled).reshape(1, 1), (1, 128)),
+        ],
+        axis=1,
+    )
+    small[r, 3:4] = sums
+    numbers = pairs(s["neighbours"][...])
+    s["high"][...] = (numbers // LO).astype(F32)
+    s["low"][...] = (numbers % LO).astype(F32)
+    s["weight"][...] = pairs(alpha)
+    mask = s["mask"]
+    flags = s["is_board"][...].astype(F32)
+    for i in range(rows // 128):
+        mask[i * 128 : (i + 1) * 128] = down(flags[i : i + 1])
+
+    pl.semaphore_wait(barrier, len(greeted))
+
+    def mask_of(q):
+        m = mask[at(q)] > 0.5
+        return jnp.concatenate([m, m], axis=1)
+
+    table, stage = s["table"], s["stage"]
+    pitch = stage.shape[0] // 64
+    pairs_piece = PIECE // 2
+
+    def piece(i):
+        iota = lax.broadcasted_iota(jnp.int32, (128, 128), 0).astype(F32).astype(BF)
+        front = lax.broadcasted_iota(jnp.int32, (16, 128), 1) < 64
+        zero, one = jnp.zeros((), BF), jnp.ones((), BF)
+
+        def tiles(v, n):
+            return jnp.concatenate([v] * n, axis=0)
+
+        def pair(j):
+            p = i * pairs_piece + j
+
+            def row(ref):
+                return jnp.broadcast_to(ref[pl.ds(p, 1), :], (16, 128))
+
+            hi, lo, al = row(s["high"]).astype(BF), row(s["low"]).astype(BF), row(s["weight"])
+            al_a = jnp.where(front, al, 0.0).astype(BF)
+            al_b = jnp.where(front, 0.0, al).astype(BF)
+            places = jnp.where(tiles(lo, 8) == iota, one, zero)
+            same = tiles(hi, 4) == iota[:64]
+            weights = jnp.concatenate(
+                [jnp.where(same, tiles(al_a, 4), zero), jnp.where(same, tiles(al_b, 4), zero)], axis=0
+            )
+            out = dot_nt(weights, places)
+            stage[pl.ds(j, 64, stride=pitch), :] = out[:64]
+            stage[pl.ds(j + pairs_piece, 64, stride=pitch), :] = out[64:]
+
+        loop(pairs_piece, pair, unroll=8)
+
+        def convert(h):
+            for f in range(2):
+                base = (2 * h + f) * pitch
+                for g in range(2):
+                    table[
+                        h,
+                        pl.ds(pl.multiple_of(i * pairs_piece + g * half, 16), pairs_piece),
+                        f * 128 : (f + 1) * 128,
+                    ] = stage[
+                        pl.ds(pl.multiple_of(base + g * pairs_piece, 8), pairs_piece), :
+                    ].astype(BF)
+
+        loop(table.shape[0], convert, unroll=4)
+
+    n_pieces = rows // PIECE
+
+    gather_b = Gather(boards, 0, s["gb_ss"], s["gb_rs"])
+    gather_h = Gather(own_h, 0, s["gh_ss"], s["gh_rs"])
+    gather_a = Gather(own_h, 4, s["ga_ss"], s["ga_rs"])
+    message, v_pre, u_pre = s["message"], s["v_pre"], s["u_pre"]
+
+    def make_h(q):
+        lines = at(q)
+        b01 = jnp.concatenate([boards[0, lines], boards[1, lines]], axis=1)
+        b23 = jnp.concatenate([boards[2, lines], boards[3, lines]], axis=1)
+        proj = dot(b01, s["proj_w"][: 2 * bwidth]) + dot(b23, s["proj_w"][2 * bwidth :]) + s["proj_b"][...]
+        own_h[c, lines] = jnp.where(mask_of(q), proj, s["pin"][lines].astype(F32)).astype(BF)
+
+    def block(zb, yb, q):
+        return message.at[zb * 2 + yb, q]
+
+    def send_up(zb, q):
+        ref = block(zb, y, q)
+        rdma(ref, ref, s["up_ss"].at[zb, q], s["msg_rs"].at[zb * 2 + y, q], ((z + 1) * 2 + y, c)).start()
+
+    def send_down(zb, q):
+        ref = block(zb, y, q)
+        rdma(ref, ref, s["down_ss"].at[zb, q], s["msg_rs"].at[zb * 2 + y, q], ((z - 1) * 2 + y, c)).start()
+
+    def send_y(zb, q):
+        ref = block(zb, y, q)
+        rdma(ref, ref, s["y_ss"].at[zb, q], s["msg_rs"].at[zb * 2 + y, q], yp).start()
+
+    def make_message(q):
+        lines = at(q)
+        acc = dot(own_h[0, lines], s["q_w"][:width])
+        for i in range(1, 4):
+            acc = acc + dot(own_h[i, lines], s["q_w"][i * width : (i + 1) * width])
+        v = acc + s["q_b"][...]
+        v_pre[lines] = v
+        message[r, q] = (v * jax.nn.sigmoid(v)).astype(BF)
+
+        @pl.when(z < 3)
+        def _():
+            send_up(z, q)
+
+        @pl.when(z > 0)
+        def _():
+            send_down(z, q)
+
+        send_y(z, q)
+
+    loop(NQ, gather_b.start)
+
+    def first_phase(t):
+        @pl.when(t < NQ)
+        def _():
+            gather_b.forward(t)
+
+        @pl.when((t >= 1) & (t < NQ + 1))
+        def _():
+            gather_b.finish(t - 1)
+            make_h(t - 1)
+            gather_h.start(t - 1)
+
+        @pl.when((t >= 2) & (t < NQ + 2))
+        def _():
+            gather_h.forward(t - 2)
+
+        @pl.when(t >= 3)
+        def _():
+            gather_h.finish(t - 3)
+            make_message(t - 3)
+
+        piece(t)
+
+    loop(NQ + 3, first_phase)
+
+    def u_from_h(q):
+        lines = at(q)
+        acc = dot(own_h[0, lines], s["w_w"][:width])
+        for i in range(1, 4):
+            acc = acc + dot(own_h[i, lines], s["w_w"][i * width : (i + 1) * width])
+        u_pre[lines] = acc + s["w_b"][...]
+
+    def second_phase(i):
+        t, q = 1 + i // NQ, i % NQ
+
+        @pl.when(z - t >= 0)
+        def _():
+            arrived(block(z - t, y, q), s["msg_rs"].at[(z - t) * 2 + y, q])
+
+            @pl.when(z < 3)
+            def _():
+                send_up(z - t, q)
+
+            send_y(z - t, q)
+
+        @pl.when(z + t <= 3)
+        def _():
+            arrived(block(z + t, y, q), s["msg_rs"].at[(z + t) * 2 + y, q])
+
+            @pl.when(z > 0)
+            def _():
+                send_down(z + t, q)
+
+            send_y(z + t, q)
+
+        @pl.when(i + NQ + 3 < n_pieces)
+        def _():
+            piece(i + NQ + 3)
+
+        @pl.when(i < NQ)
+        def _():
+            u_from_h(i)
+
+    loop(3 * NQ, second_phase)
+
+    agg = s["agg"]
+    agg[...] = jnp.zeros_like(agg)
+
+    def add_block(b):
+        def part(i):
+            lines = at(i)
+            acc = agg[lines]
+            for q in range(NQ):
+                acc = acc + dot(table[b * NQ + q, lines], message[b, q])
+            agg[lines] = acc
+
+        loop(rows // chunk, part)
+
+    loop(zn, lambda zb: add_block(zb * 2 + y))
+
+    order = [0, 1, 1, 2, 2, 3, 3]
+    signs = [1, 1, -1, 1, -1, 1, -1]
+    for t, sign in zip(order, signs):
+        zb = z + sign * t
+
+        @pl.when((zb >= 0) & (zb <= 3))
+        def _():
+            b = zb * 2 + 1 - y
+            loop(NQ, lambda q: arrived(message.at[b, q], s["msg_rs"].at[b, q]))
+            add_block(b)
+
+    own_h[4 + c] = agg[...].astype(BF)
+
+    gu, gv, gb = s["gu"], s["gv"], s["gb"]
+    stat, stat_ss, stat_rs = s["stat"], s["stat_ss"], s["stat_rs"]
+    peers = (core, xp, xk)
+
+    loop(NQ, gather_a.start)
+
+    def make_u(q):
+        lines = at(q)
+        u = u_pre[lines]
+        for i in range(4):
+            u = u + dot(own_h[4 + i, lines], s["w_w"][(4 + i) * width : (5 + i) * width])
+        u_pre[lines] = u
+        zz = u * jax.nn.sigmoid(u)
+        g = s["cotangent"][lines].astype(F32)
+        pad = jnp.zeros((4, 128), F32)
+        stat[0, q] = jnp.concatenate([row_sums(zz * zz), row_sums(g * zz), pad], axis=0)
+        for i, dev in enumerate(peers):
+            rdma(
+                stat.at[0, q], stat.at[1 + i, q], stat_ss.at[i, q], stat_rs.at[i, q], dev
+            ).start()
+
+    def make_gu(q):
+        lines = at(q)
+        for i in range(3):
+            arrived(stat.at[1 + i, q], stat_rs.at[i, q])
+        total = (stat[0, q] + stat[1, q]) + (stat[2, q] + stat[3, q])
+        rr = lax.rsqrt(total[0:2] + 1e-6)
+        scale = down_pair(rr)
+        pull = down_pair(rr * rr * rr * total[2:4])
+        u = u_pre[lines]
+        sig = jax.nn.sigmoid(u)
+        zz = u * sig
+        g = s["cotangent"][lines].astype(F32)
+        s["embeddings"][lines] = (zz * scale).astype(BF)
+        gu[lines] = ((g * scale - zz * pull) * (sig * (1.0 + u * (1.0 - sig)))).astype(BF)
+
+    def agg_part(col, q):
+        wr = s["w_w"][pl.ds(pl.multiple_of((4 + col) * width, width), width), :]
+        return dot_nt(gu[at(q)], wr)
+
+    scatter_a = Scatter(agg_part, "sa")
+    grad_agg = s["grad_agg"]
+
+    sum_w = WeightSum(lambda d, yy: dot_tn(own_h[d * 2 + yy], gu[...]), "ww", s["grad_w"])
+
+    def third_phase(t):
+        @pl.when(t < NQ)
+        def _():
+            gather_a.forward(t)
+
+        @pl.when((t >= 1) & (t < NQ + 1))
+        def _():
+            gather_a.finish(t - 1)
+            make_u(t - 1)
+
+        @pl.when((t >= 2) & (t < NQ + 2))
+        def _():
+            make_gu(t - 2)
+            scatter_a.first(t - 2)
+
+        @pl.when((t >= 3) & (t < NQ + 3))
+        def _():
+            scatter_a.second(t - 3)
+
+        @pl.when(t == NQ + 1)
+        def _():
+            sum_w.first()
+
+        @pl.when(t >= 4)
+        def _():
+            grad_agg[t - 4] = scatter_a.third(t - 4).T.astype(BF)
+
+    loop(NQ + 4, third_phase)
+
+    def sent_messages(q):
+        @pl.when(z < 3)
+        def _():
+            sent(block(z, y, q), s["up_ss"].at[z, q])
+
+        @pl.when(z > 0)
+        def _():
+            sent(block(z, y, q), s["down_ss"].at[z, q])
+
+        for t in range(1, 4):
+            @pl.when((z - t >= 0) & (z < 3))
+            def _():
+                sent(block(z, y, q), s["up_ss"].at[z - t, q])
+
+            @pl.when((z + t <= 3) & (z > 0))
+            def _():
+                sent(block(z, y, q), s["down_ss"].at[z + t, q])
+
+        for zb in range(4):
+            sent(block(z, y, q), s["y_ss"].at[zb, q])
+
+    loop(NQ, sent_messages)
+
+    ysend = lambda d, q: message.at[d, q]
+    zsend = lambda d, q: message.at[4 + d, q]
+    yrecv, zrecv = s["yrecv"], s["zrecv"]
+    m_ys, m_yr, m_zs, m_zr = s["m_ys"], s["m_yr"], s["m_zs"], s["m_zr"]
+    upper = z // 2
+    inner = z + upper * (3 - 2 * z) - 2 * upper * (z - z)
+    inner = (z % 2) + upper * (1 - 2 * (z % 2))
+    adjust = (0, 0, -1, 1)
+
+    def dest(j):
+        base = 3 - j + inner * adjust[j]
+        return base + upper * (3 - 2 * base)
+
+    def spread(d, yy, q):
+        b = (d * 2 + yy) * NQ + q
+        acc = dot(grad_agg[0], table[b, at(0)])
+        for i in range(1, NQ):
+            acc = acc + dot(grad_agg[i], table[b, at(i)])
+        return acc
+
+    for j in range(4):
+        def over_y(q, j=j):
+            d = dest(j)
+            message[d, q] = spread(d, 1 - y, q).astype(BF)
+            rdma(ysend(d, q), yrecv.at[d, q], m_ys.at[d, q], m_yr.at[d, q], yp).start()
+
+        loop(NQ, over_y)
+
+    sum_w.second()
+
+    for j in range(3):
+        d = dest(j)
+        step = 1 - 2 * upper
+        if j == 2:
+            step = step * (1 - 2 * inner)
+        is_dest = (0, inner, 1)[j]
+        slot = d + is_dest * ((1 - step) // 2) * (4 - d)
+
+        def along_z(q, d=d, step=step, slot=slot):
+            own = spread(d, y, q)
+            arrived(yrecv.at[d, q], m_yr.at[d, q])
+            message[4 + d, q] = (own + yrecv[d, q].astype(F32)).astype(BF)
+
+            @pl.when(inner == 1)
+            def _():
+                own2 = own + yrecv[d, q].astype(F32)
+                arrived(zrecv.at[d, q], m_zr.at[d, q])
+                message[4 + d, q] = (own2 + zrecv[d, q].astype(F32)).astype(BF)
+
+            rdma(
+                zsend(d, q), zrecv.at[slot, q], m_zs.at[d, q], m_zr.at[slot, q], ((z + step) * 2 + y, c)
+            ).start()
+
+        loop(NQ, along_z)
+
+    total_t = s["total_t"]
+
+    def make_gv(q):
+        own = spread(z, y, q)
+        arrived(yrecv.at[z, q], m_yr.at[z, q])
+        total_t[...] = own + yrecv[z, q].astype(F32)
+
+        @pl.when(z > 0)
+        def _():
+            arrived(zrecv.at[z, q], m_zr.at[z, q])
+            total_t[...] += zrecv[z, q].astype(F32)
+
+        @pl.when(z < 3)
+        def _():
+            arrived(zrecv.at[4, q], m_zr.at[4, q])
+            total_t[...] += zrecv[4, q].astype(F32)
+
+        v = v_pre[at(q)]
+        sig = jax.nn.sigmoid(v)
+        gv[at(q)] = (total_t[...].T * (sig * (1.0 + v * (1.0 - sig)))).astype(BF)
+
+    def h_part(col, q):
+        lines = pl.ds(pl.multiple_of(col * width, width), width)
+        return dot_nt(gu[at(q)], s["w_w"][lines, :]) + dot_nt(gv[at(q)], s["q_w"][lines, :])
+
+    def b_part(col, q):
+        lines = pl.ds(pl.multiple_of(col * bwidth, bwidth), bwidth)
+        return dot_nt(gb[at(q)], s["proj_w"][lines, :])
+
+    scatter_h, scatter_b = Scatter(h_part, "sh"), Scatter(b_part, "sb")
+
+    def q_part(d, yy):
+        return dot_tn(own_h[d, :, pl.ds(pl.multiple_of(yy * 128, 128), 128)], gv[...])
+
+    prod = s["prod"]
+
+    def p_part(d, yy):
+        prod[...] = dot_tn(boards[d], gb[...])
+        n = prod.shape[0] // 2
+        return prod[pl.ds(pl.multiple_of(yy * n, n), n), :]
+
+    sum_q = WeightSum(q_part, "wq", s["grad_q"])
+    sum_p = WeightSum(p_part, "wp", s["grad_p"])
+    small_ss, small_rs = s["small_ss"], s["small_rs"]
+
+    def send_small():
+        for i, ref in enumerate((gb, gv, gu)):
+            small[r, i : i + 1] = jnp.sum(ref[...].astype(F32), axis=0, keepdims=True)
+        for d in range(1, 8):
+            rdma(
+                small.at[r], small.at[r], small_ss.at[d - 1], small_rs.at[r], ((r + d) % 8, c)
+            ).start()
+
+    def fourth_phase(t):
+        @pl.when(t < NQ)
+        def _():
+            make_gv(t)
+            scatter_h.first(t)
+
+        @pl.when((t >= 1) & (t < NQ + 1))
+        def _():
+            scatter_h.second(t - 1)
+
+        @pl.when(t == NQ)
+        def _():
+            sum_q.first()
+
+        @pl.when((t >= 2) & (t < NQ + 2))
+        def _():
+            q = t - 2
+            g = scatter_h.third(q)
+            m = mask_of(q)
+            s["grad_pin"][at(q)] = jnp.where(m, 0.0, g)
+            gb[at(q)] = jnp.where(m, g, 0.0).astype(BF)
+            scatter_b.first(q)
+
+        @pl.when((t >= 3) & (t < NQ + 3))
+        def _():
+            scatter_b.second(t - 3)
+
+        @pl.when(t == NQ + 1)
+        def _():
+            sum_p.first()
+            send_small()
+            sum_q.second()
+
+        @pl.when(t >= 4)
+        def _():
+            s["grad_board"][at(t - 4)] = scatter_b.third(t - 4)
+
+    loop(NQ + 4, fourth_phase)
+    sum_p.second()
+    sum_w.third()
+    sum_q.third()
+    for d in range(1, 8):
+        other = (r + d) % 8
+        arrived(small.at[other], small_rs.at[other])
+    total = small[0]
+    for i in range(1, 8):
+        total = total + small[i]
+    nodes = rows * 8
+    per = jnp.concatenate(
+        [jnp.full((1, 128), 1.0 / nodes, F32), jnp.full((1, 128), 1.0 / (nodes * SLOTS), F32)], axis=1
+    )
+    s["sums"][...] = total
+    s["sums"][3:4] = total[3:4] * per
+    sum_p.third()
+
+    def drain(q):
+        gather_b.drain(q)
+        gather_h.drain(q)
+        gather_a.drain(q)
+        scatter_a.drain(q)
+        scatter_h.drain(q)
+        scatter_b.drain(q)
+        for i in range(3):
+            sent(stat.at[0, q], stat_ss.at[i, q])
+        for d in range(4):
+            sent(ysend(d, q), m_ys.at[d, q])
+
+            @pl.when(d != z)
+            def _():
+                sent(zsend(d, q), m_zs.at[d, q])
+
+    loop(NQ, drain)
+    sum_w.drain()
+    sum_q.drain()
+    sum_p.drain()
+    for d in range(7):
+        sent(small.at[r], small_ss.at[d])
+
+
+def fused_device(
+    pin, board, is_board, neighbours, present, importance, proj_w, proj_b, q_w, q_b, w_w, w_b, cotangent
+):
+    rows, width = pin.shape
+    bwidth = board.shape[1]
+    chunk = rows // NQ
+    nodes = rows * 8
+    inputs = dict(
+        pin=pin,
+        board=board,
+        is_board=is_board.reshape(rows // 128, 128),
+        neighbours=neighbours,
+        present=present,
+        importance=importance,
+        proj_w=proj_w,
+        proj_b=proj_b.reshape(1, width),
+        q_w=q_w,
+        q_b=q_b.reshape(1, width),
+        w_w=w_w,
+        w_b=w_b.reshape(1, width),
+        cotangent=cotangent,
+    )
+    shape = jax.ShapeDtypeStruct
+    outs = dict(
+        embeddings=shape((rows, width), BF),
+        grad_pin=shape((rows, width), F32),
+        grad_board=shape((rows, bwidth), F32),
+        grad_p=shape((bwidth * 4 // 8, width), F32),
+        grad_q=shape((width * 4 // 8, width), F32),
+        grad_w=shape((2 * width * 4 // 8, width), F32),
+        sums=shape((8, width), F32),
+    )
+    vmem, dma = pltpu.VMEM, pltpu.SemaphoreType.DMA
+    scratch = dict(
+        table=vmem((nodes // chunk, rows, chunk), BF),
+        stage=vmem((64 * (PIECE + 8), 128), F32),
+        high=vmem((rows // 2, 128), F32),
+        low=vmem((rows // 2, 128), F32),
+        weight=vmem((rows // 2, 128), F32),
+        mask=vmem((rows, 128), F32),
+        boards=vmem((4, rows, bwidth), BF),
+        ha=vmem((8, rows, width), BF),
+        message=vmem((8, NQ, chunk, width), BF),
+        v_pre=vmem((rows, width), F32),
+        u_pre=vmem((rows, width), F32),
+        agg=vmem((rows, width), F32),
+        gu=vmem((rows, width), BF),
+        gv=vmem((rows, width), BF),
+        gb=vmem((rows, width), BF),
+        grad_agg=vmem((NQ, width, chunk), BF),
+        stat=vmem((4, NQ, 8, 128), F32),
+        small=vmem((8, 8, width), F32),
+        yrecv=vmem((4, NQ, width, chunk), BF),
+        zrecv=vmem((5, NQ, width, chunk), BF),
+        total_t=vmem((width, chunk), F32),
+        prod=vmem((bwidth, width), F32),
+        stat_ss=dma((3, NQ)),
+        stat_rs=dma((3, NQ)),
+        msg_rs=dma((8, NQ)),
+        up_ss=dma((4, NQ)),
+        down_ss=dma((4, NQ)),
+        y_ss=dma((4, NQ)),
+        m_ys=dma((4, NQ)),
+        m_yr=dma((4, NQ)),
+        m_zs=dma((4, NQ)),
+        m_zr=dma((5, NQ)),
+        small_ss=dma((7,)),
+        small_rs=dma((8,)),
+    )
+    for name in ("gb", "gh", "ga"):
+        scratch[name + "_ss"] = dma((3, NQ))
+        scratch[name + "_rs"] = dma((3, NQ))
+    for name, w in (("sa", width), ("sh", width), ("sb", bwidth)):
+        scratch[name + "_send1"] = vmem((2, NQ, chunk, w), BF)
+        scratch[name + "_recv1"] = vmem((2, NQ, chunk, w), BF)
+        scratch[name + "_sendx"] = vmem((NQ, chunk, w), BF)
+        scratch[name + "_recvx"] = vmem((NQ, chunk, w), BF)
+        scratch[name + "_ss"] = dma((3, NQ))
+        scratch[name + "_rs"] = dma((3, NQ))
+    for name, n in (("ww", width), ("wq", width // 2), ("wp", bwidth // 2)):
+        for part in ("_ysend", "_yrecv", "_zsend", "_zrecv"):
+            scratch[name + part] = vmem((4, n, width), BF)
+        scratch[name + "_ss"] = dma((2, 4))
+        scratch[name + "_rs"] = dma((2, 4))
+    whole = pl.BlockSpec(memory_space=pltpu.VMEM)
+    got = pl.pallas_call(
+        functools.partial(fused_kernel, names=tuple(inputs) + tuple(outs) + tuple(scratch)),
+        out_shape=list(outs.values()),
+        in_specs=[whole] * len(inputs),
+        out_specs=[whole] * len(outs),
+        scratch_shapes=list(scratch.values()),
+        compiler_params=pltpu.CompilerParams(
+            collective_id=1, has_side_effects=True, vmem_limit_bytes=62 << 20
+        ),
+        cost_estimate=pl.CostEstimate(flops=14 << 30, bytes_accessed=8 << 20, transcendentals=0),
+    )(*inputs.values())
+    emb, g_pin, g_board, g_proj, g_q, g_w, sums = got
+    return (
+        emb,
+        g_pin,
+        g_board,
+        g_proj,
+        sums[0],
+        g_q,
+        sums[1],
+        g_w,
+        sums[2],
+        sums[3, 0],
+        sums[3, 128],
+    )
 
 
 def silu_slope(value):
@@ -240,6 +1055,7 @@
         P(),
         P(),
     )
+    fused = mesh.shape["rows"] == 8 and mesh.shape["cols"] == 4
     return jax.shard_map(
-        per_device, mesh=mesh, in_specs=in_specs, out_specs=out_specs, check_vma=False
-    )
+        fused_device if fused else per_device, mesh=mesh, in_specs=in_specs, out_specs=out_specs, check_vma=False
+    )

time: 1340 us -> 192 us (0.14)
  other arithmetic: 617 us -> 0 us
  waiting for transfers between devices: 475 us -> 0 us
  Pallas kernels: 0 us -> 178 us
  matrix products: 125 us -> 0 us
  local copies, waits for them, and re-layouts: 54.7 us -> 12.8 us
  blocking collectives: 26.2 us -> 0 us
  loops' own time: 24.1 us -> 0 us
  between operations: 17.7 us -> 0.68 us
    reduce_sum x20 -> x0, other arithmetic: 609 us -> none  [the longest x16 603 us: slot_table(): jnp.sum(jnp.where(offsets[:, :, None] == places, alpha_block[:, :, None],...]
    reduce_scatter x5 -> x0, waiting for transfers between devices: 278 us -> none  [the longest x1 84.4 us: per_device(): lax.psum_scatter(table.astype(jnp.bfloat16), 'rows', scatter_dimension=0,...]
    pallas_call x0 -> x1, Pallas kernels: none -> 178 us  [fused_device(): pl.pallas_call(functools.partial(fused_kernel, names=tuple(inputs) + tupl...]
    all_gather x4 -> x0, waiting for transfers between devices: 132 us -> none  [the longest x1 71.6 us: per_device(): message_all = lax.all_gather(message, 'rows', axis=0, tiled=True)]
    dot_general x44 -> x0, matrix products: 125 us -> none  [the longest x8 35.3 us: step(): jnp.dot(lower, piece, preferred_element_type=jnp.float32)]
    unnamed x13 -> x0, waiting for transfers between devices: 65.5 us -> none
    psum x2 -> x0, blocking collectives: 26.2 us -> none  [the longest x1 20.2 us: per_device(): lax.psum((bias_terms[0], bias_terms[1], bias_terms[2]), 'rows')]
    another operation x8 -> x0, loops' own time: 24.1 us -> none  [the longest x2 21 us: one_rows(): lax.scan(step, jnp.zeros((row_block, columns), jnp.float32), jnp.arange(c...]
  transfers between devices with their start and end apart: 11 -> 0, of which waited for: 11 -> 0; matrix products, arithmetic and copies ran while one was open for 2% -> 0% of each run, Pallas kernels for 0% -> 0%
where the time goes in v1:
time: 192 us
  Pallas kernels  178 us (93%)
  local copies, waits for them, and re-layouts  12.8 us (7%)
    pallas_call x1, Pallas kernels, fused_device(): pl.pallas_call(functools.partial(fused_kernel, names=tuple(inputs) + tupl...  178 us
    unnamed x23, local copies, waits for them, and re-layouts  10.1 us

profile of v1, /device:TPU:0, one launch (start us, length us, event | category | flops | bytes accessed | tf_op | source)
XLA Modules:
  0.0 191.6 jit_solution(9101666704998442)
XLA Ops:
  0.6 0.0 copy-start.3
  0.7 2.0 %copy.24.refs_3_ = s32[1024,50]{1,0:T(8,128)} copy(s32[1024,50]{0,1:T(8,128)} %param.16) | data formatting | bytes 409600 | tf_op args[3]
  2.6 0.0 copy-done.3
  2.6 0.0 copy-start.4
  2.6 1.0 copy.25.refs_4_
  3.7 0.0 copy-done.4
  3.7 1.0 copy.26.refs_5_
  4.7 178.1 %shard_map.212 = (bf16[1024,256]{1,0:T(8,128)(2,1)}, f32[1024,256]{1,0:T(8,128)}, f32[1024,128]{1,0:T(8,128)}, f32[64,256]{1,0:T(8,128)}, f32[128,256]{1,0:T(8,1...) custom-call(bf16[1024,256]{1,0:T(8,128)(2,1)} %refs_0_.1, bf16[1024,128]{1,0:T(8,128)(2,1)} %refs_1_.1, s32[8,128]{1,0:T(8,128)} %bitcast.12, ...), custom_call_target="tpu_custom_call" | custom-call | flops 15032385536 | bytes 8388608 | tf_op jit(solution)/shard_map/pallas_call | solution.py:799
  182.8 0.0 copy-start
  182.8 1.3 fusion
  184.1 1.4 fusion.1
  185.5 1.9 copy.33
  187.3 0.0 copy-done
  187.3 0.0 copy-start.1
  187.3 1.0 copy.34
  188.3 0.4 copy-done.1
  188.7 0.0 copy-start.6
  188.7 0.0 copy-start.5
  188.7 0.8 copy.35
  189.5 0.1 copy-done.6
  189.6 0.0 copy-start.2
  189.6 0.6 copy.36
  190.2 0.0 copy-done.5
  190.2 0.7 copy.37
  190.9 0.0 copy-done.2
  190.9 0.7 copy.38
Async XLA Ops:
  0.6 2.0 %copy-start.3 = (s32[1024,50]{0,1:T(8,128)S(1)}, s32[1024,50]{0,1:T(8,128)}, u32[]{:S(2)}) copy-start(s32[1024,50]{0,1:T(8,128)} %param.17) | copy-start | bytes 614404
  2.6 1.0 copy-start.4
  182.8 4.6 %copy-start = (f32[1024,256]{1,0:T(8,128)S(1)}, f32[1024,256]{1,0:T(8,128)}, u32[]{:S(2)}) copy-start(f32[1024,256]{1,0:T(8,128)} %get-tuple-element.42) | copy-start | bytes 3145732
  187.3 1.4 copy-start.1
  188.7 0.9 copy-start.6
  188.7 1.5 copy-start.5
  189.6 1.3 copy-start.2

commit v2 on v1

v2 whole, which is shorter than its diff:
```python
import functools
import math
import types

import jax
import jax.numpy as jnp
from jax import lax
from jax.experimental import pallas as pl
from jax.experimental.pallas import tpu as pltpu
from jax.sharding import PartitionSpec as P

SLOTS = 50
MESH = pl.DeviceIdType.MESH
BF = jnp.bfloat16
F32 = jnp.float32
NQ = 4
NP = 2
LO_BITS = 7
LO = 1 << LO_BITS
PIECE = 64
NT = (((1,), (1,)), ((), ()))
TN = (((0,), (0,)), ((), ()))


def dot(a, b):
    return jnp.dot(a, b, preferred_element_type=F32)


def dot_nt(a, b):
    return lax.dot_general(a, b, NT, preferred_element_type=F32)


def dot_tn(a, b):
    return lax.dot_general(a, b, TN, preferred_element_type=F32)


def loop(n, body, unroll=1):
    def step(i, carry):
        body(i)
        return carry

    lax.fori_loop(0, n, step, 0, unroll=unroll)


def row_sums(x):
    y = x[:, :128] + x[:, 128:]
    sums = [
        jnp.sum(y[i * 128 : (i + 1) * 128].T, axis=0, keepdims=True) for i in range(x.shape[0] // 128)
    ]
    return sums[0] if len(sums) == 1 else jnp.concatenate(sums, axis=0)


def down(row):
    return jnp.broadcast_to(row, (128, 128)).T


def down_rows(rows):
    cols = [down(rows[i : i + 1]) for i in range(rows.shape[0])]
    col = cols[0] if len(cols) == 1 else jnp.concatenate(cols, axis=0)
    return jnp.concatenate([col, col], axis=1)


def fused_kernel(*refs, names):
    s = types.SimpleNamespace(**dict(zip(names, refs)))
    r = lax.axis_index("rows")
    c = lax.axis_index("cols")
    z, y = r // 2, r % 2
    x, k = c // 2, c % 2
    rows, width = s.pin.shape
    bwidth = s.boards.shape[2]
    chunk = rows // NQ
    zn = 4
    per_block = rows // LO
    core = (r, x * 2 + 1 - k)
    xp = (r, (1 - x) * 2 + k)
    xk = (r, (1 - x) * 2 + 1 - k)
    yp = (z * 2 + 1 - y, c)
    upper = z // 2
    inner = (z % 2) + upper * (1 - 2 * (z % 2))
    zx = z + 1 - 2 * (z % 2)
    zxp = (zx * 2 + y, c)

    def at(q):
        return pl.ds(pl.multiple_of(q * chunk, chunk), chunk)

    def rdma(src, dst, send, recv, dev):
        return pltpu.make_async_remote_copy(
            src_ref=src, dst_ref=dst, send_sem=send, recv_sem=recv, device_id=dev, device_id_type=MESH
        )

    def arrived(ref, sem):
        rdma(ref, ref, sem, sem, core).wait_recv()

    def sent(ref, sem):
        rdma(ref, ref, sem, sem, core).wait_send()

    class Gather:
        def __init__(self, buf, base, ss, rs):
            self.buf, self.base, self.ss, self.rs = buf, base, ss, rs

        def ref(self, col, q):
            return self.buf.at[self.base + col, at(q)]

        def start(self, q):
            own = self.ref(c, q)
            rdma(own, own, self.ss.at[1, q], self.rs.at[1, q], xp).start()
            rdma(own, own, self.ss.at[0, q], self.rs.at[0, q], core).start()

        def forward(self, q):
            got = self.ref((1 - x) * 2 + k, q)
            arrived(got, self.rs.at[1, q])
            rdma(got, got, self.ss.at[2, q], self.rs.at[2, q], core).start()

        def finish(self, q):
            arrived(self.ref(x * 2 + 1 - k, q), self.rs.at[0, q])
            arrived(self.ref((1 - x) * 2 + 1 - k, q), self.rs.at[2, q])

        def drain(self, q):
            for i in range(3):
                sent(self.ref(c, q), self.ss.at[i, q])

    class Scatter:
        def __init__(self, part, name):
            self.part = part
            self.send1, self.recv1 = getattr(s, name + "_send1"), getattr(s, name + "_recv1")
            self.sendx, self.recvx = getattr(s, name + "_sendx"), getattr(s, name + "_recvx")
            self.ss, self.rs = getattr(s, name + "_ss"), getattr(s, name + "_rs")

        def first(self, q):
            for i, xs in ((0, 1 - x), (1, x)):
                self.send1[i, q] = self.part(xs * 2 + 1 - k, q).astype(BF)
                rdma(
                    self.send1.at[i, q], self.recv1.at[i, q], self.ss.at[i, q], self.rs.at[i, q], core
                ).start()

        def second(self, q):
            own = self.part((1 - x) * 2 + k, q)
            arrived(self.recv1.at[0, q], self.rs.at[0, q])
            self.sendx[q] = (own + self.recv1[0, q].astype(F32)).astype(BF)
            rdma(self.sendx.at[q], self.recvx.at[q], self.ss.at[2, q], self.rs.at[2, q], xp).start()

        def third(self, q):
            own = self.part(c, q)
            arrived(self.recv1.at[1, q], self.rs.at[1, q])
            own = own + self.recv1[1, q].astype(F32)
            arrived(self.recvx.at[q], self.rs.at[2, q])
            return own + self.recvx[q].astype(F32)

        def drain(self, q):
            for i in range(2):
                sent(self.send1.at[i, q], self.ss.at[i, q])
            sent(self.sendx.at[q], self.ss.at[2, q])

    class WeightSum:
        def __init__(self, part, name, out, ysend, zsend):
            self.part, self.out = part, out
            self.ysend, self.zsend = ysend, zsend
            self.yrecv, self.zrecv = getattr(s, name + "_yrecv"), getattr(s, name + "_zrecv")
            self.ss, self.rs = getattr(s, name + "_ss"), getattr(s, name + "_rs")

        def first(self):
            def step(d):
                ref = self.ysend(d)
                ref[...] = self.part(d, 1 - y).astype(BF)
                rdma(ref, self.yrecv.at[d], self.ss.at[0, d], self.rs.at[0, d], yp).start()

            loop(zn, step)

        def second(self):
            def step(d):
                own = self.part(d, y)
                arrived(self.yrecv.at[d], self.rs.at[0, d])
                own = own + self.yrecv[d].astype(F32)

                @pl.when(d == z)
                def _():
                    self.out[...] = own

                @pl.when(d != z)
                def _():
                    ref = self.zsend(d)
                    ref[...] = own.astype(BF)
                    rdma(
                        ref, self.zrecv.at[z], self.ss.at[1, d], self.rs.at[1, z], (d * 2 + y, c)
                    ).start()

            loop(zn, step)

        def third(self):
            def step(d):
                @pl.when(d != z)
                def _():
                    arrived(self.zrecv.at[d], self.rs.at[1, d])
                    self.out[...] += self.zrecv[d].astype(F32)

            loop(zn, step)

        def drain(self):
            def step(d):
                sent(self.ysend(d), self.ss.at[0, d])

                @pl.when(d != z)
                def _():
                    sent(self.zsend(d), self.ss.at[1, d])

            loop(zn, step)

    class DirectSum:
        def __init__(self, out):
            self.out, self.send, self.recv = out, s.wp_send, s.wp_recv
            self.ss, self.rs = s.wp_ss, s.wp_rs

        def first(self, part):
            n = self.out.shape[0]

            def step(d):
                both = part(d)
                for yy in range(2):
                    block = both[yy * n : (yy + 1) * n]
                    row = d * 2 + yy

                    @pl.when(row == r)
                    def _():
                        self.out[...] = block

                    @pl.when(row != r)
                    def _():
                        ref = self.send.at[row]
                        ref[...] = block.astype(BF)
                        rdma(ref, self.recv.at[r], self.ss.at[row], self.rs.at[r], (row, c)).start()

            loop(zn, step)

        def second(self):
            def step(row):
                @pl.when(row != r)
                def _():
                    arrived(self.recv.at[row], self.rs.at[row])
                    self.out[...] += self.recv[row].astype(F32)

            loop(2 * zn, step)

        def drain(self):
            def step(row):
                @pl.when(row != r)
                def _():
                    sent(self.send.at[row], self.ss.at[row])

            loop(2 * zn, step)

    barrier = pltpu.get_barrier_semaphore()
    greeted = [(r, (c + d) % 4) for d in range(1, 4)] + [((r + d) % 8, c) for d in range(1, 8)]
    for dev in greeted:
        pl.semaphore_signal(barrier, inc=1, device_id=dev, device_id_type=MESH)

    boards, own_h = s.boards, s.ha
    in_sem = s.in_sem
    loads = {}
    order = (
        ("board", boards.at[c]),
        ("is_board", s.flags),
        ("proj_w", s.proj_w),
        ("proj_b", s.proj_b),
        ("pin", s.pin),
        ("neighbours", s.numbers),
        ("present", s.present),
        ("importance", s.importance),
        ("q_w", s.q_w),
        ("q_b", s.q_b),
        ("w_w", s.w_w),
        ("w_b", s.w_b),
        ("cotangent", s.cotangent),
    )
    for i, (name, ref) in enumerate(order):
        loads[name] = pltpu.make_async_copy(getattr(s, name + "_in"), ref, in_sem.at[i])
        loads[name].start()

    out_sem = s.out_sem

    def store(i, q, src, dst):
        return pltpu.make_async_copy(src, dst, out_sem.at[i, q])

    gather_b = Gather(boards, 0, s.gb_ss, s.gb_rs)
    gather_h = Gather(own_h, 0, s.gh_ss, s.gh_rs)
    loads["board"].wait()
    pl.semaphore_wait(barrier, len(greeted))
    loop(NQ, gather_b.start)

    mask = s.mask
    loads["is_board"].wait()
    flags = s.flags[...].astype(F32)
    for i in range(rows // 128):
        mask[i * 128 : (i + 1) * 128] = down(flags[i : i + 1])

    half = rows // 2
    padded = s.padded
    list_ss, list_rs = s.list_ss, s.list_rs

    quarter = rows // 4

    def lay(ref):
        for t in range(2):
            for i in range(quarter // 128):
                a, b = 2 * t * quarter + i * 128, (2 * t + 1) * quarter + i * 128
                ref[t, i * 128 : (i + 1) * 128] = jnp.concatenate(
                    [padded[:, a : a + 128], padded[:, b : b + 128]], axis=0
                ).T

    def lend_list(i):
        src, dst = ((s.numbers, s.numbers2), (s.alpha, s.alpha2))[i]
        return rdma(src, dst, list_ss.at[i], list_rs.at[i], yp)

    def prepare():
        for name in ("neighbours", "present", "importance"):
            loads[name].wait()
        lend_list(0).start()
        present = s.present[...].astype(F32)
        filled = present * s.importance[...]
        padded[SLOTS:] = jnp.zeros((padded.shape[0] - SLOTS, rows), F32)
        padded[:SLOTS] = filled / jnp.sum(filled, axis=0, keepdims=True)
        s.alpha[...] = padded[...].astype(BF)
        lend_list(1).start()
        lay(s.weight)
        small = s.small
        small[r] = jnp.zeros(small.shape[1:], F32)
        small[r, 3:4] = jnp.concatenate(
            [
                jnp.broadcast_to(jnp.sum(present).reshape(1, 1), (1, 128)),
                jnp.broadcast_to(jnp.sum(filled).reshape(1, 1), (1, 128)),
            ],
            axis=1,
        )
        numbers = s.numbers[...]
        padded[:SLOTS] = (numbers >> LO_BITS).astype(F32)
        lay(s.high)
        padded[:SLOTS] = (numbers & (LO - 1)).astype(F32)
        lay(s.low)

    def prepare2():
        for i in range(2):
            lend_list(i).wait_recv()
        numbers = s.numbers2[...]
        high = numbers >> LO_BITS
        place = (high // (2 * per_block)) * per_block + high % per_block
        padded[:SLOTS] = jnp.where((high // per_block) % 2 == y, place, -1).astype(F32)
        lay(s.high2)
        padded[:SLOTS] = (numbers & (LO - 1)).astype(F32)
        lay(s.low2)
        padded[...] = s.alpha2[...].astype(F32)
        lay(s.weight2)

    def mask_of(q):
        m = mask[at(q)] > 0.5
        return jnp.concatenate([m, m], axis=1)

    table, stage = s.table, s.stage
    pitch = stage.shape[0] // 64
    piece_rows = PIECE // 4

    def build(i, lists, table):
        n_high = 2 * table.shape[0]
        iota = lax.broadcasted_iota(jnp.int32, (128, 128), 0).astype(F32).astype(BF)
        front = lax.broadcasted_iota(jnp.int32, (16, 128), 1) < 64
        zero, one = jnp.zeros((), BF), jnp.ones((), BF)

        def tiles(v, n):
            return jnp.concatenate([v] * n, axis=0)

        zeros = jnp.zeros((n_high, 128), BF)
        n = n_high // 16

        def four(j):
            p = i * piece_rows + j
            weights, places = [], []
            for t in range(2):

                def row(ref):
                    return jnp.broadcast_to(ref[t, pl.ds(p, 1), :], (16, 128))

                hi, lo, al = row(lists[0]).astype(BF), row(lists[1]).astype(BF), row(lists[2])
                places.append(jnp.where(tiles(lo, 8) == iota, one, zero))
                same = tiles(hi, n) == iota[:n_high]
                for a in (jnp.where(front, al, 0.0), jnp.where(front, 0.0, al)):
                    w = jnp.where(same, tiles(a.astype(BF), n), zero)
                    weights.append(jnp.concatenate([w, zeros] if t == 0 else [zeros, w], axis=1))
            out = dot_nt(jnp.concatenate(weights, axis=0), jnp.concatenate(places, axis=1))
            for g in range(4):
                stage[pl.ds(j + g * piece_rows, n_high, stride=pitch), :] = out[
                    g * n_high : (g + 1) * n_high
                ]

        loop(piece_rows, four, unroll=16)

        def convert(h):
            for f in range(2):
                base = (2 * h + f) * pitch
                for g in range(4):
                    table[
                        h,
                        pl.ds(pl.multiple_of(i * piece_rows + g * quarter, 16), piece_rows),
                        f * 128 : (f + 1) * 128,
                    ] = stage[
                        pl.ds(pl.multiple_of(base + g * piece_rows, 8), piece_rows), :
                    ].astype(BF)

        loop(table.shape[0], convert, unroll=4)

    lists1 = (s.high, s.low, s.weight)
    lists2 = (s.high2, s.low2, s.weight2)
    table2 = s.table2

    def piece(i):
        build(i, lists1, table)

    def piece2(i):
        build(i, lists2, table2)

    n_pieces = rows // PIECE

    message, v_pre = s.message, s.v_pre

    def make_h(q):
        lines = at(q)
        b01 = jnp.concatenate([boards[0, lines], boards[1, lines]], axis=1)
        b23 = jnp.concatenate([boards[2, lines], boards[3, lines]], axis=1)
        proj = dot(b01, s.proj_w[: 2 * bwidth]) + dot(b23, s.proj_w[2 * bwidth :]) + s.proj_b[...]
        own_h[c, lines] = jnp.where(mask_of(q), proj, s.pin[lines].astype(F32)).astype(BF)

    def block(zb, yb, q):
        return message.at[zb * 2 + yb, q]

    def send_up(zb, q):
        ref = block(zb, y, q)
        rdma(ref, ref, s.up_ss.at[zb, q], s.msg_rs.at[zb * 2 + y, q], ((z + 1) * 2 + y, c)).start()

    def send_down(zb, q):
        ref = block(zb, y, q)
        rdma(ref, ref, s.down_ss.at[zb, q], s.msg_rs.at[zb * 2 + y, q], ((z - 1) * 2 + y, c)).start()

    def send_y(zb, q):
        ref = block(zb, y, q)
        rdma(ref, ref, s.y_ss.at[zb, q], s.msg_rs.at[zb * 2 + y, q], yp).start()

    def make_message(q):
        lines = at(q)
        acc = dot(own_h[0, lines], s.q_w[:width])
        for i in range(1, 4):
            acc = acc + dot(own_h[i, lines], s.q_w[i * width : (i + 1) * width])
        v = acc + s.q_b[...]
        v_pre[lines] = v
        message[r, q] = (v * jax.nn.sigmoid(v)).astype(BF)

        @pl.when(z < 3)
        def _():
            send_up(z, q)

        @pl.when(z > 0)
        def _():
            send_down(z, q)

        send_y(z, q)

    prepare()
    for name in ("proj_w", "proj_b", "pin"):
        loads[name].wait()

    def board_phase(q):
        gather_b.forward(q)
        gather_b.finish(q)
        make_h(q)
        gather_h.start(q)

    piece(0)
    loop(NQ, board_phase)
    early = 3
    loop(early - 1, lambda i: piece(1 + i))

    half = rows // 2
    sub = half // NP
    own_half = pl.ds(pl.multiple_of(x * half, half), half)
    their_half = pl.ds(pl.multiple_of((1 - x) * half, half), half)
    lend_ss, lend_rs = s.lend_ss, s.lend_rs
    wide = 4 * width

    def lends():
        return (
            (s.w_w.at[:wide], s.w2.at[:wide]),
            (s.w_b, s.w_b2),
            (s.w_w.at[wide:], s.w2.at[wide:]),
            (s.cotangent.at[their_half], s.cotangent2),
        )

    def lend(i):
        src, dst = lends()[i]
        return rdma(src, dst, lend_ss.at[i], lend_rs.at[i], xp)

    for name in ("w_w", "w_b", "cotangent"):
        loads[name].wait()
    for i in range(4):
        lend(i).start()
    loads["q_w"].wait()
    loads["q_b"].wait()

    def message_phase(q):
        gather_h.forward(q)
        gather_h.finish(q)
        make_message(q)
        piece(early + q)

        @pl.when(q % 2 == 0)
        def _():
            piece(early + NQ + q // 2)

    loop(NQ, message_phase)
    built = early + NQ + NQ // 2

    u_pre = s.u_pre

    def part_of(i):
        return pl.ds(pl.multiple_of(i * sub, sub), sub)

    def mine(i):
        return pl.ds(pl.multiple_of(x * half + i * sub, sub), sub)

    def theirs(i):
        return pl.ds(pl.multiple_of((1 - x) * half + i * sub, sub), sub)

    def u_from_h(i):
        for n, w, b in ((0, s.w_w, s.w_b), (1, s.w2, s.w_b2)):
            acc = dot(own_h[0, mine(i)], w[:width])
            for m in range(1, 4):
                acc = acc + dot(own_h[m, mine(i)], w[m * width : (m + 1) * width])
            u_pre[n, part_of(i)] = acc + b[...]

    agg = s.grad_pin
    parts = rows // chunk

    def add(b, first, n):
        for i in range(parts):
            lines = slice(i * chunk, (i + 1) * chunk)
            acc = agg[lines]
            for q in range(first, first + n):
                acc = acc + dot(table[b * NQ + q, lines], message[b, q])
            agg[lines] = acc

    def over_y(zb, q):
        @pl.when((zb != zx) | ((inner == 0) & (q < NQ // 2)))
        def _():
            send_y(zb, q)

    def send_zx(q):
        ref = block(z, 1 - y, q)
        rdma(ref, ref, s.zx_ss.at[q], s.msg_rs.at[z * 2 + 1 - y, q], zxp).start()

    def at_z(zb):
        return (zb >= 0) & (zb <= 3)

    n_second = 3 * NQ
    n_second2 = n_pieces // 2
    steps = n_pieces - built

    def second_phase(i):
        t, q = 1 + i // NQ, i % NQ

        @pl.when(z - t >= 0)
        def _():
            arrived(block(z - t, y, q), s.msg_rs.at[(z - t) * 2 + y, q])

            @pl.when(z < 3)
            def _():
                send_up(z - t, q)

            over_y(z - t, q)

        @pl.when(z + t <= 3)
        def _():
            arrived(block(z + t, y, q), s.msg_rs.at[(z + t) * 2 + y, q])

            @pl.when(z > 0)
            def _():
                send_down(z + t, q)

            over_y(z + t, q)

        @pl.when(t == 1)
        def _():
            arrived(block(z, 1 - y, q), s.msg_rs.at[z * 2 + 1 - y, q])

            @pl.when(inner == 0)
            def _():
                send_zx(q)

        @pl.when((t == 3) & (inner == 1) & (q >= NQ // 2))
        def _():
            send_zx(q)

        @pl.when(i < steps)
        def _():
            piece(built + i)

        @pl.when(i == 0)
        def _():
            prepare2()

        @pl.when((i > 0) & (i < 1 + n_second2))
        def _():
            loop(2, lambda n: piece2(2 * (i - 1) + n))

        @pl.when(i == steps)
        def _():
            agg[...] = jnp.zeros_like(agg)
            lend(0).wait_recv()
            lend(1).wait_recv()

        @pl.when(i >= n_second - NP)
        def _():
            u_from_h(i - (n_second - NP))

        @pl.when((i >= n_second - 5) & (i < n_second))
        def _():
            n = i - (n_second - 5)
            zb = z + jnp.where(n == 0, 0, jnp.where(n == 1, -1, jnp.where(n == 2, 1, jnp.where(n == 3, -2, 2))))

            @pl.when(at_z(zb))
            def _():
                add(zb * 2 + y, 0, NQ)

    loop(n_second, second_phase)

    add(z * 2 + 1 - y, 0, NQ)
    for zb in (z - 3, z + 3):
        @pl.when(at_z(zb))
        def _():
            add(zb * 2 + y, 0, NQ)

    def add_arriving(zb, first, n):
        b = zb * 2 + 1 - y
        loop(n, lambda q: arrived(message.at[b, first + q], s.msg_rs.at[b, first + q]))
        add(b, first, n)

    add_arriving(zx, 0, NQ // 2)
    for t in (1, 2, 3):
        for zb in (z - t, z + t):
            @pl.when(at_z(zb) & (zb != zx))
            def _():
                add_arriving(zb, 0, NQ)

    add_arriving(zx, NQ // 2, NQ // 2)
    own_h[4 + c] = agg[...].astype(BF)

    gu, gv, gb, gu2 = s.gu, s.gv, s.gb, s.gu2
    stat, stat_ss, stat_rs = s.stat, s.stat_ss, s.stat_rs
    ga_ss, ga_rs = s.ga_ss, s.ga_rs
    other_x = (1 - x) * 2 + k

    def agg_ref(col, lines):
        return own_h.at[4 + col, lines]

    def agg_start(i):
        a, b = agg_ref(c, theirs(i)), agg_ref(c, mine(i))
        rdma(a, a, ga_ss.at[1, i], ga_rs.at[1, i], xp).start()
        rdma(b, b, ga_ss.at[0, i], ga_rs.at[0, i], core).start()

    def agg_forward(i):
        got = agg_ref(other_x, mine(i))
        arrived(got, ga_rs.at[1, i])
        rdma(got, got, ga_ss.at[2, i], ga_rs.at[2, i], core).start()

    def agg_finish(i):
        arrived(agg_ref(x * 2 + 1 - k, mine(i)), ga_rs.at[0, i])
        arrived(agg_ref((1 - x) * 2 + 1 - k, mine(i)), ga_rs.at[2, i])

    def rest_start():
        a, b = agg_ref(c, own_half), agg_ref(c, their_half)
        rdma(a, a, ga_ss.at[1, NP], ga_rs.at[1, NP], xp).start()
        rdma(b, b, ga_ss.at[0, NP], ga_rs.at[0, NP], core).start()

    def rest_forward():
        got = agg_ref(other_x, their_half)
        arrived(got, ga_rs.at[1, NP])
        rdma(got, got, ga_ss.at[2, NP], ga_rs.at[2, NP], core).start()

    def rest_finish():
        arrived(agg_ref(x * 2 + 1 - k, their_half), ga_rs.at[0, NP])
        arrived(agg_ref((1 - x) * 2 + 1 - k, their_half), ga_rs.at[2, NP])

    loop(NP, agg_start)
    lend(2).wait_recv()
    lend(3).wait_recv()

    def gradients(i):
        return s.cotangent[mine(i)].astype(F32), s.cotangent2[part_of(i)].astype(F32)

    def make_u(i):
        us = [u_pre[n, part_of(i)] for n in range(2)]
        for m in range(4):
            a = own_h[4 + m, mine(i)]
            us = [u + dot(a, w[(4 + m) * width : (5 + m) * width]) for u, w in zip(us, (s.w_w, s.w2))]
        squares, inners = 0.0, 0.0
        for n, (u, g) in enumerate(zip(us, gradients(i))):
            u_pre[n, part_of(i)] = u
            zz = u * jax.nn.sigmoid(u)
            squares = squares + zz * zz
            inners = inners + g * zz
        pad = jnp.zeros((8 - 2 * sub // 128, 128), F32)
        stat[0, i] = jnp.concatenate([row_sums(squares), row_sums(inners), pad], axis=0)
        rdma(stat.at[0, i], stat.at[1, i], stat_ss.at[i], stat_rs.at[i], core).start()

    def make_gu(i):
        arrived(stat.at[1, i], stat_rs.at[i])
        total = stat[0, i] + stat[1, i]
        n_rows = sub // 128
        rr = lax.rsqrt(total[:n_rows] + 1e-6)
        scale = down_rows(rr)
        pull = down_rows(rr * rr * rr * total[n_rows : 2 * n_rows])
        for n, (g, emb, grad) in enumerate(
            zip(gradients(i), (s.embeddings, s.emb2), (gu, gu2))
        ):
            u = u_pre[n, part_of(i)]
            sig = jax.nn.sigmoid(u)
            zz = u * sig
            lines = mine(i) if n == 0 else part_of(i)
            emb[lines] = (zz * scale).astype(BF)
            grad[lines] = ((g * scale - zz * pull) * (sig * (1.0 + u * (1.0 - sig)))).astype(BF)

    def agg_part(col, i):
        lines = pl.ds(pl.multiple_of((4 + col) * width, width), width)
        return dot_nt(gu[mine(i)], s.w_w[lines, :]) + dot_nt(gu2[part_of(i)], s.w2[lines, :])

    grad_agg, grad_agg2 = s.grad_agg, s.grad_agg2
    sa_send, sa_recv, sa_x, sa_ss, sa_rs = s.sa_send, s.sa_recv, s.sa_x, s.sa_ss, s.sa_rs

    def agg_first(i):
        for n, xs in ((0, 1 - x), (1, x)):
            sa_send[n, i] = agg_part(xs * 2 + 1 - k, i).astype(BF)
            rdma(sa_send.at[n, i], sa_recv.at[n, i], sa_ss.at[n, i], sa_rs.at[n, i], core).start()

    def agg_second(i):
        own = agg_part(other_x, i)
        arrived(sa_recv.at[0, i], sa_rs.at[0, i])
        sa_x[i] = (own + sa_recv[0, i].astype(F32)).T.astype(BF)
        rdma(sa_x.at[i], grad_agg.at[x * NP + i], sa_ss.at[2, i], sa_rs.at[2, i], xp).start()

    def agg_third(i):
        own = agg_part(c, i)
        arrived(sa_recv.at[1, i], sa_rs.at[1, i])
        grad_agg[x * NP + i] = (own + sa_recv[1, i].astype(F32)).T.astype(BF)
        agg_over_y(x * NP + i)

    def agg_over_y(i):
        rdma(grad_agg.at[i], grad_agg2.at[i], s.gy_ss.at[i], s.gy_rs.at[i], yp).start()

    def room(at_block, n):
        return [lambda d, b=b, n=n: message.at[b, d, pl.ds(0, n)] for b in (at_block, at_block + 1)]

    def room_narrow(at_block, n):
        return [lambda d, i=i: message.at[at_block, d, pl.ds(i * n, n)] for i in range(2)]

    sum_w = WeightSum(lambda d, yy: dot_tn(own_h[d * 2 + yy], gu[...]), "ww", s.grad_w, *room(4, width))

    def third_phase(t):
        @pl.when(t < NP)
        def _():
            agg_forward(t)
            agg_finish(t)
            make_u(t)

        @pl.when((t >= 2) & (t < NP + 2))
        def _():
            agg_second(t - 2)
            agg_third(t - 2)

        @pl.when((t >= 1) & (t < NP + 1))
        def _():
            make_gu(t - 1)
            agg_first(t - 1)

    loop(NP + 2, third_phase)

    def give(n):
        src, dst = ((gu2, gu.at[own_half]), (s.emb2, s.embeddings.at[own_half]))[n]
        return rdma(src, dst, s.give_ss.at[n], s.give_rs.at[n], xp)

    def give_back(n):
        ref = (gu, s.embeddings)[n].at[their_half]
        return rdma(ref, ref, s.give_ss.at[n], s.give_rs.at[n], xp)

    give(0).start()
    rest_start()
    give(1).start()
    def pass_on(i):
        arrived(grad_agg.at[(1 - x) * NP + i], sa_rs.at[2, i])
        agg_over_y((1 - x) * NP + i)

    loop(NP, pass_on)
    loop(2 * NP, lambda i: arrived(grad_agg2.at[i], s.gy_rs.at[i]))

    def sent_messages(q):
        @pl.when(z < 3)
        def _():
            sent(block(z, y, q), s.up_ss.at[z, q])

        @pl.when(z > 0)
        def _():
            sent(block(z, y, q), s.down_ss.at[z, q])

        for t in range(1, 4):
            @pl.when((z - t >= 0) & (z < 3))
            def _():
                sent(block(z, y, q), s.up_ss.at[z - t, q])

            @pl.when((z + t <= 3) & (z > 0))
            def _():
                sent(block(z, y, q), s.down_ss.at[z + t, q])

        for zb in range(4):
            @pl.when((zb != zx) | ((inner == 0) & (q < NQ // 2)))
            def _():
                sent(block(z, y, q), s.y_ss.at[zb, q])

        @pl.when((inner == 0) | (q >= NQ // 2))
        def _():
            sent(block(z, y, q), s.zx_ss.at[q])

    loop(NQ, sent_messages)

    zsend, zrecv = message, s.zrecv
    m_zs, m_zr = s.m_zs, s.m_zr
    adjust = (0, 0, -1, 1)

    def dest(j):
        base = 3 - j + inner * adjust[j]
        return base + upper * (3 - 2 * base)

    each = 2 * NP // NQ

    def sum_of(terms):
        total = None
        for term in terms:
            total = term if total is None else total + term
        return total

    def spread(d, q):
        own, other = (d * 2 + y) * NQ + q, d * NQ + q

        def grads(ref, i):
            return jnp.concatenate([ref[m] for m in range(i * each, (i + 1) * each)], axis=1)

        return sum_of(
            dot(grads(ref, i), tab[b, at(i)])
            for ref, tab, b in ((grad_agg, table, own), (grad_agg2, table2, other))
            for i in range(NQ)
        )

    def along(j):
        d = dest(j)
        step = 1 - 2 * upper
        if j == 2:
            step = step * (1 - 2 * inner)
        is_dest = (0, inner, 1)[j]
        slot = d + is_dest * ((1 - step) // 2) * (4 - d)

        def along_z(q):
            own = spread(d, q)

            @pl.when(inner == 0)
            def _():
                zsend[d, q] = own.astype(BF)

            @pl.when(inner == 1)
            def _():
                arrived(zrecv.at[d, q], m_zr.at[d, q])
                zsend[d, q] = (own + zrecv[d, q].astype(F32)).astype(BF)

            rdma(
                zsend.at[d, q], zrecv.at[slot, q], m_zs.at[d, q], m_zr.at[slot, q], ((z + step) * 2 + y, c)
            ).start()

        loop(NQ, along_z)

    along(0)

    @pl.when(inner == 0)
    def _():
        along(1)
        along(2)

    for n in range(2):
        give_back(n).wait_recv()
    store(0, 0, s.embeddings, s.embeddings_out).start()
    rest_forward()
    rest_finish()
    sum_w.first()

    @pl.when(inner == 1)
    def _():
        along(1)
        along(2)

    sum_w.second()

    total_t = s.total_t

    def make_gv(q):
        total_t[...] = spread(z, q)

        @pl.when(z > 0)
        def _():
            arrived(zrecv.at[z, q], m_zr.at[z, q])
            total_t[...] += zrecv[z, q].astype(F32)

        @pl.when(z < 3)
        def _():
            arrived(zrecv.at[4, q], m_zr.at[4, q])
            total_t[...] += zrecv[4, q].astype(F32)

        v = v_pre[at(q)]
        sig = jax.nn.sigmoid(v)
        gv[at(q)] = (total_t[...].T * (sig * (1.0 + v * (1.0 - sig)))).astype(BF)

    def h_part(col, q):
        lines = pl.ds(pl.multiple_of(col * width, width), width)
        return dot_nt(gu[at(q)], s.w_w[lines, :]) + dot_nt(gv[at(q)], s.q_w[lines, :])

    def b_part(col, q):
        lines = pl.ds(pl.multiple_of(col * bwidth, bwidth), bwidth)
        return dot_nt(gb[at(q)], s.proj_w[lines, :])

    scatter_h, scatter_b = Scatter(h_part, "sh"), Scatter(b_part, "sb")

    def q_part(d, yy):
        return dot_tn(own_h[d, :, pl.ds(pl.multiple_of(yy * 128, 128), 128)], gv[...])

    sum_q = WeightSum(q_part, "wq", s.grad_q, *room_narrow(6, width // 2))
    sum_p = DirectSum(s.grad_p)
    small, small_ss, small_rs = s.small, s.small_ss, s.small_rs

    def send_small():
        for i, ref in enumerate((gb, gv, gu)):
            small[r, i : i + 1] = jnp.sum(ref[...].astype(F32), axis=0, keepdims=True)
        for d in range(1, 8):
            rdma(
                small.at[r], small.at[r], small_ss.at[d - 1], small_rs.at[r], ((r + d) % 8, c)
            ).start()

    def finish_board(q):
        s.grad_board[at(q)] = scatter_b.third(q)
        store(2, q, s.grad_board.at[at(q)], s.grad_board_out.at[at(q)]).start()

    def fourth_phase(t):
        @pl.when(t < NQ)
        def _():
            make_gv(t)
            scatter_h.first(t)

        @pl.when((t >= 2) & (t < NQ + 2))
        def _():
            q = t - 2
            g = scatter_h.third(q)
            m = mask_of(q)
            gb[at(q)] = jnp.where(m, g, 0.0).astype(BF)
            s.grad_pin[at(q)] = jnp.where(m, 0.0, g)

            @pl.when(t == NQ + 1)
            def _():
                sum_p.first(lambda d: dot_tn(boards[d], gb[...]))

            scatter_b.first(q)
            store(1, q, s.grad_pin.at[at(q)], s.grad_pin_out.at[at(q)]).start()

        @pl.when(t < NQ)
        def _():
            scatter_h.second(t)

        @pl.when(t == NQ - 1)
        def _():
            sum_q.first()

        @pl.when(t == NQ + 1)
        def _():
            send_small()

        @pl.when((t >= 2) & (t < NQ + 2))
        def _():
            scatter_b.second(t - 2)

        @pl.when(t == NQ + 1)
        def _():
            sum_q.second()

        @pl.when(t >= NQ)
        def _():
            finish_board(t - NQ)

    loop(NQ + 2, fourth_phase)
    sum_w.third()
    store(0, 1, s.grad_w, s.grad_w_out).start()
    loop(NQ - 2, lambda t: finish_board(t + 2))
    sum_q.third()
    store(0, 2, s.grad_q, s.grad_q_out).start()
    for d in range(1, 8):
        other = (r + d) % 8
        arrived(small.at[other], small_rs.at[other])
    total = small[0]
    for i in range(1, 8):
        total = total + small[i]
    nodes = rows * 8
    per = jnp.concatenate(
        [jnp.full((1, 128), 1.0 / nodes, F32), jnp.full((1, 128), 1.0 / (nodes * SLOTS), F32)], axis=1
    )
    s.sums[...] = total
    s.sums[3:4] = total[3:4] * per
    store(0, 3, s.sums, s.sums_out).start()
    sum_p.second()
    store(3, 0, s.grad_p, s.grad_p_out).start()

    def drain(q):
        gather_b.drain(q)
        gather_h.drain(q)
        scatter_h.drain(q)
        scatter_b.drain(q)
        store(1, q, s.grad_pin.at[at(q)], s.grad_pin_out.at[at(q)]).wait()
        store(2, q, s.grad_board.at[at(q)], s.grad_board_out.at[at(q)]).wait()
        for d in range(4):
            @pl.when(d != z)
            def _():
                sent(zsend.at[d, q], m_zs.at[d, q])

    loop(NQ, drain)

    def drain_half(i):
        for n in range(3):
            sent(agg_ref(c, mine(i)), ga_ss.at[n, i])
        for n in range(2):
            sent(sa_send.at[n, i], sa_ss.at[n, i])
        sent(sa_x.at[i], sa_ss.at[2, i])
        sent(stat.at[0, i], stat_ss.at[i])

    loop(NP, drain_half)
    for n in range(3):
        sent(agg_ref(c, own_half), ga_ss.at[n, NP])
    for n in range(4):
        lend(n).wait_send()
    for n in range(2):
        lend_list(n).wait_send()
    loop(2 * NP, lambda i: sent(grad_agg.at[i], s.gy_ss.at[i]))
    for n in range(2):
        give(n).wait_send()
    sum_w.drain()
    sum_q.drain()
    sum_p.drain()
    for d in range(7):
        sent(small.at[r], small_ss.at[d])
    for i, (n, name) in enumerate(
        ((0, "embeddings"), (0, "grad_w"), (0, "grad_q"), (0, "sums"), (3, "grad_p"))
    ):
        store(n, i % 4, getattr(s, name), getattr(s, name + "_out")).wait()


def finish_kernel(*refs):
    ins, sums, outs, small, held, sem = refs[:6], refs[6], refs[7:13], refs[13:18], refs[18:24], refs[24]
    first = [pltpu.make_async_copy(a, b, sem.at[0, i]) for i, (a, b) in enumerate(zip(ins, held))]
    second = [pltpu.make_async_copy(a, b, sem.at[1, i]) for i, (a, b) in enumerate(zip(held, outs))]
    for copy in first:
        copy.start()
    for i in range(3):
        small[i][...] = sums[i : i + 1]
    small[3][...] = sums[3:4, 0:1]
    small[4][...] = sums[3:4, 128:129]
    for a, b in zip(first, second):
        a.wait()
        b.start()
    for copy in second:
        copy.wait()


def fused_device(
    pin, board, is_board, neighbours, present, importance, proj_w, proj_b, q_w, q_b, w_w, w_b, cotangent
):
    rows, width = pin.shape
    bwidth = board.shape[1]
    chunk = rows // NQ
    nodes = rows * 8
    inputs = dict(
        board=board,
        is_board=is_board.reshape(rows // 128, 128),
        proj_w=proj_w,
        proj_b=proj_b.reshape(1, width),
        pin=pin,
        neighbours=neighbours.T,
        present=present.T,
        importance=importance.T,
        q_w=q_w,
        q_b=q_b.reshape(1, width),
        w_w=w_w,
        w_b=w_b.reshape(1, width),
        cotangent=cotangent,
    )
    shape = jax.ShapeDtypeStruct
    outs = dict(
        embeddings=shape((rows, width), BF),
        grad_pin=shape((rows, width), F32),
        grad_board=shape((rows, bwidth), F32),
        grad_p=shape((bwidth * 4 // 8, width), F32),
        grad_q=shape((width * 4 // 8, width), F32),
        grad_w=shape((2 * width * 4 // 8, width), F32),
        sums=shape((8, width), F32),
    )
    vmem, dma = pltpu.VMEM, pltpu.SemaphoreType.DMA
    scratch = dict(
        in_sem=dma((len(inputs),)),
        out_sem=dma((4, NQ)),
        flags=vmem((rows // 128, 128), jnp.int32),
        numbers=vmem((SLOTS, rows), jnp.int32),
        numbers2=vmem((SLOTS, rows), jnp.int32),
        alpha=vmem((64, rows), BF),
        alpha2=vmem((64, rows), BF),
        padded=vmem((64, rows), F32),
        table2=vmem((nodes // 2 // chunk, rows, chunk), BF),
        high2=vmem((2, rows // 4, 128), F32),
        low2=vmem((2, rows // 4, 128), F32),
        weight2=vmem((2, rows // 4, 128), F32),
        grad_agg2=vmem((2 * NP, width, rows // 2 // NP), BF),
        table=vmem((nodes // chunk, rows, chunk), BF),
        stage=vmem((64 * (PIECE + 8), 128), F32),
        high=vmem((2, rows // 4, 128), F32),
        low=vmem((2, rows // 4, 128), F32),
        weight=vmem((2, rows // 4, 128), F32),
        mask=vmem((rows, 128), F32),
        boards=vmem((4, rows, bwidth), BF),
        ha=vmem((8, rows, width), BF),
        message=vmem((8, NQ, chunk, width), BF),
        v_pre=vmem((rows, width), F32),
        u_pre=vmem((2, rows // 2, width), F32),
        w2=vmem(w_w.shape, BF),
        w_b2=vmem((1, width), F32),
        cotangent2=vmem((rows // 2, width), BF),
        gu2=vmem((rows // 2, width), BF),
        emb2=vmem((rows // 2, width), BF),
        sa_send=vmem((2, NP, rows // 2 // NP, width), BF),
        sa_recv=vmem((2, NP, rows // 2 // NP, width), BF),
        sa_x=vmem((NP, width, rows // 2 // NP), BF),
        sa_ss=dma((3, NP)),
        sa_rs=dma((3, NP)),
        ga_ss=dma((3, NP + 1)),
        ga_rs=dma((3, NP + 1)),
        lend_ss=dma((4,)),
        lend_rs=dma((4,)),
        give_ss=dma((2,)),
        give_rs=dma((2,)),
        gu=vmem((rows, width), BF),
        gv=vmem((rows, width), BF),
        gb=vmem((rows, width), BF),
        grad_agg=vmem((2 * NP, width, rows // 2 // NP), BF),
        stat=vmem((2, NP, 8, 128), F32),
        small=vmem((8, 8, width), F32),
        zrecv=vmem((5, NQ, width, chunk), BF),
        total_t=vmem((width, chunk), F32),
        stat_ss=dma((NP,)),
        stat_rs=dma((NP,)),
        msg_rs=dma((8, NQ)),
        up_ss=dma((4, NQ)),
        down_ss=dma((4, NQ)),
        y_ss=dma((4, NQ)),
        zx_ss=dma((NQ,)),
        m_zs=dma((4, NQ)),
        m_zr=dma((5, NQ)),
        list_ss=dma((2,)),
        list_rs=dma((2,)),
        gy_ss=dma((2 * NP,)),
        gy_rs=dma((2 * NP,)),
        small_ss=dma((7,)),
        small_rs=dma((8,)),
    )
    for name in ("present", "importance", "proj_w", "proj_b", "pin", "q_w", "q_b", "w_w", "w_b", "cotangent"):
        scratch[name] = vmem(inputs[name].shape, inputs[name].dtype)
    for name, out in outs.items():
        scratch[name] = vmem(out.shape, out.dtype)
    for name in ("gb", "gh"):
        scratch[name + "_ss"] = dma((3, NQ))
        scratch[name + "_rs"] = dma((3, NQ))
    for name, w in (("sh", width), ("sb", bwidth)):
        scratch[name + "_send1"] = vmem((2, NQ, chunk, w), BF)
        scratch[name + "_recv1"] = vmem((2, NQ, chunk, w), BF)
        scratch[name + "_sendx"] = vmem((NQ, chunk, w), BF)
        scratch[name + "_recvx"] = vmem((NQ, chunk, w), BF)
        scratch[name + "_ss"] = dma((3, NQ))
        scratch[name + "_rs"] = dma((3, NQ))
    for name, n in (("ww", width), ("wq", width // 2)):
        for part in ("_yrecv", "_zrecv"):
            scratch[name + part] = vmem((4, n, width), BF)
        scratch[name + "_ss"] = dma((2, 4))
        scratch[name + "_rs"] = dma((2, 4))
    for name in ("wp_send", "wp_recv"):
        scratch[name] = vmem((8, bwidth // 2, width), BF)
    for name in ("wp_ss", "wp_rs"):
        scratch[name] = dma((8,))
    place = pl.BlockSpec(memory_space=pl.ANY)
    whole = pl.BlockSpec(memory_space=pltpu.VMEM)
    names = [n + "_in" for n in inputs] + [n + "_out" for n in outs] + list(scratch)
    got = pl.pallas_call(
        functools.partial(fused_kernel, names=tuple(names)),
        out_shape=list(outs.values()),
        in_specs=[place] * len(inputs),
        out_specs=[place] * len(outs),
        scratch_shapes=list(scratch.values()),
        compiler_params=pltpu.CompilerParams(
            collective_id=1, has_side_effects=True, vmem_limit_bytes=63 << 20
        ),
        cost_estimate=pl.CostEstimate(flops=14 << 30, bytes_accessed=8 << 20, transcendentals=0),
    )(*inputs.values())
    row, one = shape((1, width), F32), shape((1, 1), F32)
    emb, g_pin, g_board, g_proj, g_q, g_w, p_b, q_bias, w_bias, count, weight = pl.pallas_call(
        finish_kernel,
        out_shape=list(outs.values())[:6] + [row, row, row, one, one],
        in_specs=[place] * 6 + [whole],
        out_specs=[place] * 6 + [whole] * 5,
        scratch_shapes=[vmem(out.shape, out.dtype) for out in list(outs.values())[:6]] + [dma((2, 6))],
        cost_estimate=pl.CostEstimate(flops=0, bytes_accessed=5 << 20, transcendentals=0),
    )(*got)
    return (
        emb,
        g_pin,
        g_board,
        g_proj,
        p_b.reshape(width),
        g_q,
        q_bias.reshape(width),
        g_w,
        w_bias.reshape(width),
        count.reshape(()),
        weight.reshape(()),
    )


def silu_slope(value):
    sig = jax.nn.sigmoid(value)
    return sig * (1.0 + value * (1.0 - sig))


def slot_table(nbr_block, alpha_block, start, width):
    offsets = nbr_block - start
    places = lax.broadcasted_iota(jnp.int32, (1, 1, width), 2)
    return jnp.sum(jnp.where(offsets[:, :, None] == places, alpha_block[:, :, None], 0.0), axis=1)


def split_pair(table):
    upper = table.astype(jnp.bfloat16)
    lower = (table - upper.astype(jnp.float32)).astype(jnp.bfloat16)
    return (upper, lower)


def collect_rows(nbrs, alphas, table_all):
    total, columns = table_all.shape
    col_tile = math.gcd(total, 2048)
    count_tiles = total // col_tile
    tiles = table_all.reshape(count_tiles, col_tile, columns)
    rows = nbrs.shape[0]
    row_block = math.gcd(rows, 512)
    count_rows = rows // row_block

    def one_rows(pair):
        nbr_block, alpha_block = pair

        def step(acc, index):
            upper, lower = split_pair(
                slot_table(nbr_block, alpha_block, index * col_tile, col_tile)
            )
            piece = tiles[index]
            acc = acc + jnp.dot(upper, piece, preferred_element_type=jnp.float32)
            return (acc + jnp.dot(lower, piece, preferred_element_type=jnp.float32), None)

        acc, unused = lax.scan(
            step, jnp.zeros((row_block, columns), jnp.float32), jnp.arange(count_tiles)
        )
        return acc

    out = lax.map(
        one_rows,
        (nbrs.reshape(count_rows, row_block, -1), alphas.reshape(count_rows, row_block, -1)),
    )
    return out.reshape(rows, columns)


def spread_rows(grads, nbrs, alphas, base, width):
    rows, columns = grads.shape
    row_block = math.gcd(rows, 512)
    count_rows = rows // row_block
    col_tile = math.gcd(width, 2048)
    count_tiles = width // col_tile
    stacked = (
        grads.reshape(count_rows, row_block, columns),
        nbrs.reshape(count_rows, row_block, -1),
        alphas.reshape(count_rows, row_block, -1),
    )
    tdot = (((0,), (0,)), ((), ()))

    def one_tile(index):

        def step(acc, triple):
            grad_block, nbr_block, alpha_block = triple
            upper, lower = split_pair(
                slot_table(nbr_block, alpha_block, base + index * col_tile, col_tile)
            )
            acc = acc + lax.dot_general(upper, grad_block, tdot, preferred_element_type=jnp.float32)
            return (
                acc + lax.dot_general(lower, grad_block, tdot, preferred_element_type=jnp.float32),
                None,
            )

        acc, unused = lax.scan(step, jnp.zeros((col_tile, columns), jnp.float32), stacked)
        return acc

    out = lax.map(one_tile, jnp.arange(count_tiles))
    return out.reshape(width, columns)


def per_device(
    pin_features,
    board_features,
    is_board,
    neighbours,
    present,
    importance,
    proj_weight,
    proj_bias,
    q_weight,
    q_bias,
    w_weight,
    w_bias,
    cotangent,
):
    local_rows = pin_features.shape[0]
    width = q_weight.shape[0]
    filled = present.astype(jnp.float32) * importance
    alpha = filled / jnp.sum(filled, axis=1, keepdims=True)
    board_mask = (is_board == 1)[:, None]
    stat_terms = (jnp.sum(present.astype(jnp.float32)), jnp.sum(filled))
    stat_totals = lax.psum((stat_terms[0], stat_terms[1]), "rows")
    board_full = lax.all_gather(board_features, "cols", axis=1, tiled=True)
    board_proj = jnp.dot(board_full, proj_weight, preferred_element_type=jnp.float32) + proj_bias
    h_local = jnp.where(board_mask, board_proj, pin_features.astype(jnp.float32)).astype(
        jnp.bfloat16
    )
    h_full = lax.all_gather(h_local, "cols", axis=1, tiled=True)
    v_pre = jnp.dot(h_full, q_weight, preferred_element_type=jnp.float32) + q_bias
    message = jax.nn.silu(v_pre).astype(jnp.bfloat16)
    message_all = lax.all_gather(message, "rows", axis=0, tiled=True)
    agg_local = collect_rows(neighbours, alpha, message_all).astype(jnp.bfloat16)
    agg_full = lax.all_gather(agg_local, "cols", axis=1, tiled=True)
    w_self = w_weight[:width]
    w_agg = w_weight[width:]
    u_pre = (
        jnp.dot(h_full, w_self, preferred_element_type=jnp.float32)
        + jnp.dot(agg_full, w_agg, preferred_element_type=jnp.float32)
        + w_bias
    )
    z_act = jax.nn.silu(u_pre)
    squares = lax.psum(jnp.sum(z_act * z_act, axis=1), "cols")
    scale = lax.rsqrt(squares + 1e-06)[:, None]
    embeddings = (z_act * scale).astype(jnp.bfloat16)
    grad_out = cotangent.astype(jnp.float32)
    inner = lax.psum(jnp.sum(grad_out * z_act, axis=1), "cols")[:, None]
    grad_z = grad_out * scale - z_act * scale * scale * scale * inner
    grad_u = (grad_z * silu_slope(u_pre)).astype(jnp.bfloat16)
    agg_part = lax.dot_general(
        grad_u, w_agg, (((1,), (1,)), ((), ())), preferred_element_type=jnp.float32
    )
    grad_agg = lax.psum_scatter(agg_part, "cols", scatter_dimension=1, tiled=True).astype(
        jnp.bfloat16
    )
    table = spread_rows(grad_agg, neighbours, alpha, 0, message_all.shape[0])
    grad_message = lax.psum_scatter(
        table.astype(jnp.bfloat16), "rows", scatter_dimension=0, tiled=True
    ).astype(jnp.float32)
    grad_v = (grad_message * silu_slope(v_pre)).astype(jnp.bfloat16)
    h_part = lax.dot_general(
        grad_u, w_self, (((1,), (1,)), ((), ())), preferred_element_type=jnp.float32
    )
    h_part = h_part + lax.dot_general(
        grad_v, q_weight, (((1,), (1,)), ((), ())), preferred_element_type=jnp.float32
    )
    grad_h = lax.psum_scatter(
        h_part.astype(jnp.bfloat16), "cols", scatter_dimension=1, tiled=True
    ).astype(jnp.float32)
    grad_pin = jnp.where(board_mask, 0.0, grad_h)
    grad_hb = jnp.where(board_mask, grad_h, 0.0).astype(jnp.bfloat16)
    board_part = lax.dot_general(
        grad_hb, proj_weight, (((1,), (1,)), ((), ())), preferred_element_type=jnp.float32
    )
    grad_board = lax.psum_scatter(
        board_part.astype(jnp.bfloat16), "cols", scatter_dimension=1, tiled=True
    ).astype(jnp.float32)
    tdot = (((0,), (0,)), ((), ()))
    grad_w_local = jnp.concatenate(
        [
            lax.dot_general(h_full, grad_u, tdot, preferred_element_type=jnp.float32),
            lax.dot_general(agg_full, grad_u, tdot, preferred_element_type=jnp.float32),
        ],
        axis=0,
    )
    grad_q_local = lax.dot_general(h_full, grad_v, tdot, preferred_element_type=jnp.float32)
    grad_p_local = lax.dot_general(board_full, grad_hb, tdot, preferred_element_type=jnp.float32)
    grad_w, grad_q, grad_proj = (
        lax.psum_scatter(
            grad_w_local.astype(jnp.bfloat16), "rows", scatter_dimension=0, tiled=True
        ).astype(jnp.float32),
        lax.psum_scatter(
            grad_q_local.astype(jnp.bfloat16), "rows", scatter_dimension=0, tiled=True
        ).astype(jnp.float32),
        lax.psum_scatter(
            grad_p_local.astype(jnp.bfloat16), "rows", scatter_dimension=0, tiled=True
        ).astype(jnp.float32),
    )
    bias_terms = (
        jnp.sum(grad_hb.astype(jnp.float32), axis=0),
        jnp.sum(grad_v.astype(jnp.float32), axis=0),
        jnp.sum(grad_u.astype(jnp.float32), axis=0),
    )
    grad_pb, grad_qb, grad_wb = lax.psum((bias_terms[0], bias_terms[1], bias_terms[2]), "rows")
    all_nodes = local_rows * lax.axis_size("rows")
    mean_count = stat_totals[0] / all_nodes
    mean_weight = stat_totals[1] / (all_nodes * SLOTS)
    return (
        embeddings,
        grad_pin,
        grad_board,
        grad_proj,
        grad_pb,
        grad_q,
        grad_qb,
        grad_w,
        grad_wb,
        mean_count,
        mean_weight,
    )


def solution(mesh):
    in_specs = (
        P("rows", "cols"),
        P("rows", "cols"),
        P("rows"),
        P("rows", None),
        P("rows", None),
        P("rows", None),
        P(None, "cols"),
        P("cols"),
        P(None, "cols"),
        P("cols"),
        P(None, "cols"),
        P("cols"),
        P("rows", "cols"),
    )
    out_specs = (
        P("rows", "cols"),
        P("rows", "cols"),
        P("rows", "cols"),
        P("rows", "cols"),
        P("cols"),
        P("rows", "cols"),
        P("cols"),
        P("rows", "cols"),
        P("cols"),
        P(),
        P(),
    )
    fused = mesh.shape["rows"] == 8 and mesh.shape["cols"] == 4
    return jax.shard_map(
        fused_device if fused else per_device, mesh=mesh, in_specs=in_specs, out_specs=out_specs, check_vma=False
    )
```

time: 192 us -> 160 us (0.83)
  Pallas kernels: 178 us -> 159 us
  local copies, waits for them, and re-layouts: 12.8 us -> 0 us
    pallas_call x1 -> x2, Pallas kernels: 178 us -> 159 us  [the longest x1 154 us: fused_device(): pl.pallas_call(functools.partial(fused_kernel, names=tuple(names)), out_s...]
    unnamed x23 -> x0, local copies, waits for them, and re-layouts: 10.1 us -> none
    slice x2 -> x0, local copies, waits for them, and re-layouts: 2.68 us -> none  [the longest x1 1.38 us: fused_device(): sums[2]]
where the time goes in v2:
time: 160 us; the launch traced here: 159 us
  Pallas kernels  159 us (99%)
    pallas_call x1, Pallas kernels, fused_device(): pl.pallas_call(functools.partial(fused_kernel, names=tuple(names)), out_s...  154 us
    pallas_call x1, Pallas kernels, fused_device(): pl.pallas_call(finish_kernel, out_shape=list(outs.values())[:6] + [row, r...  4.06 us

profile of v2, /device:TPU:0, one launch (start us, length us, event | category | flops | bytes accessed | tf_op | source)
XLA Modules:
  0.0 159.4 jit_solution(5795766608797139911)
XLA Ops:
  0.6 154.5 %shard_map.212 = (bf16[1024,256]{1,0:T(8,128)(2,1)}, f32[1024,256]{1,0:T(8,128)}, f32[1024,128]{1,0:T(8,128)}, f32[64,256]{1,0:T(8,128)}, f32[128,256]{1,0:T(8,1...) custom-call(bf16[1024,128]{1,0:T(8,128)(2,1)} %refs_0_.1, s32[8,128]{1,0:T(8,128)} %bitcast.15, bf16[512,256]{1,0:T(8,128)(2,1)} %refs_2_.1, ...), custom_call_target="tpu_custom_call" | custom-call | flops 15032385536 | bytes 8388608 | tf_op jit(solution)/shard_map/pallas_call | solution.py:1201
  155.1 4.1 %shard_map.213 = (bf16[1024,256]{1,0:T(8,128)(2,1)}, f32[1024,256]{1,0:T(8,128)}, f32[1024,128]{1,0:T(8,128)}, f32[64,256]{1,0:T(8,128)}, f32[128,256]{1,0:T(8,1...) custom-call(bf16[1024,256]{1,0:T(8,128)(2,1)} %get-tuple-element.29., ...), custom_call_target="tpu_custom_call" | custom-call | bytes 5242880 | tf_op jit(solution)/shard_map/pallas_call | solution.py:1213

commit v3 on v2

--- a/solution.py
+++ b/solution.py
@@ -73,7 +73,7 @@
     per_block = rows // LO
     core = (r, x * 2 + 1 - k)
     xp = (r, (1 - x) * 2 + k)
-    xk = (r, (1 - x) * 2 + 1 - k)
+    diagonal = (z * 2 + 1 - y, (1 - x) * 2 + k)
     yp = (z * 2 + 1 - y, c)
     upper = z // 2
     inner = (z % 2) + upper * (1 - 2 * (z % 2))
@@ -161,13 +161,14 @@
         def first(self):
             def step(d):
                 ref = self.ysend(d)
-                ref[...] = self.part(d, 1 - y).astype(BF)
+                ref[...] = self.part(d, 1 - y, True).astype(BF)
                 rdma(ref, self.yrecv.at[d], self.ss.at[0, d], self.rs.at[0, d], yp).start()
 
-            loop(zn, step)
-
-        def second(self):
-            def step(d):
+            loop(zn, step, unroll=zn)
+
+        def second(self, at0=0, n=4):
+            def step(i):
+                d = at0 + i
                 own = self.part(d, y)
                 arrived(self.yrecv.at[d], self.rs.at[0, d])
                 own = own + self.yrecv[d].astype(F32)
@@ -184,7 +185,7 @@
                         ref, self.zrecv.at[z], self.ss.at[1, d], self.rs.at[1, z], (d * 2 + y, c)
                     ).start()
 
-            loop(zn, step)
+            loop(n, step)
 
         def third(self):
             def step(d):
@@ -249,9 +250,21 @@
             loop(2 * zn, step)
 
     barrier = pltpu.get_barrier_semaphore()
-    greeted = [(r, (c + d) % 4) for d in range(1, 4)] + [((r + d) % 8, c) for d in range(1, 8)]
-    for dev in greeted:
+
+    def greet(dev):
         pl.semaphore_signal(barrier, inc=1, device_id=dev, device_id_type=MESH)
+
+    near_by = (xp, yp, diagonal, core)
+    for dev in near_by:
+        greet(dev)
+
+    @pl.when(z < 3)
+    def _():
+        greet(((z + 1) * 2 + y, c))
+
+    @pl.when(z > 0)
+    def _():
+        greet(((z - 1) * 2 + y, c))
 
     boards, own_h = s.boards, s.ha
     in_sem = s.in_sem
@@ -283,7 +296,7 @@
     gather_b = Gather(boards, 0, s.gb_ss, s.gb_rs)
     gather_h = Gather(own_h, 0, s.gh_ss, s.gh_rs)
     loads["board"].wait()
-    pl.semaphore_wait(barrier, len(greeted))
+    pl.semaphore_wait(barrier, len(near_by) + 1 + inner)
     loop(NQ, gather_b.start)
 
     mask = s.mask
@@ -628,10 +641,10 @@
     loop(n_second, second_phase)
 
     add(z * 2 + 1 - y, 0, NQ)
-    for zb in (z - 3, z + 3):
-        @pl.when(at_z(zb))
-        def _():
-            add(zb * 2 + y, 0, NQ)
+
+    @pl.when(inner == 0)
+    def _():
+        add((3 - z) * 2 + y, 0, NQ)
 
     def add_arriving(zb, first, n):
         b = zb * 2 + 1 - y
@@ -639,14 +652,20 @@
         add(b, first, n)
 
     add_arriving(zx, 0, NQ // 2)
-    for t in (1, 2, 3):
-        for zb in (z - t, z + t):
-            @pl.when(at_z(zb) & (zb != zx))
-            def _():
-                add_arriving(zb, 0, NQ)
-
-    add_arriving(zx, NQ // 2, NQ // 2)
-    own_h[4 + c] = agg[...].astype(BF)
+    add_arriving(2 - upper, 0, NQ)
+    for q in range(NQ):
+        blocks = [3 * (1 - upper) * 2 + 1 - y] + ([zx * 2 + 1 - y] if q >= NQ // 2 else [])
+        for b in blocks:
+            arrived(message.at[b, q], s.msg_rs.at[b, q])
+        for i in range(parts):
+            lines = slice(i * chunk, (i + 1) * chunk)
+            acc = agg[lines]
+            for b in blocks:
+                acc = acc + dot(table[b * NQ + q, lines], message[b, q])
+            if q < NQ - 1:
+                agg[lines] = acc
+            else:
+                own_h[4 + c, lines] = acc.astype(BF)
 
     gu, gv, gb, gu2 = s.gu, s.gv, s.gb, s.gu2
     stat, stat_ss, stat_rs = s.stat, s.stat_ss, s.stat_rs
@@ -739,6 +758,9 @@
         own = agg_part(other_x, i)
         arrived(sa_recv.at[0, i], sa_rs.at[0, i])
         sa_x[i] = (own + sa_recv[0, i].astype(F32)).T.astype(BF)
+        if i == NP - 1:
+            to, there = grad_agg2.at[x * NP + i], (1 - x) * NP + i
+            rdma(sa_x.at[i], to, s.gy_ss.at[there], s.gy_rs.at[x * NP + i], diagonal).start()
         rdma(sa_x.at[i], grad_agg.at[x * NP + i], sa_ss.at[2, i], sa_rs.at[2, i], xp).start()
 
     def agg_third(i):
@@ -756,26 +778,25 @@
     def room_narrow(at_block, n):
         return [lambda d, i=i: message.at[at_block, d, pl.ds(i * n, n)] for i in range(2)]
 
-    sum_w = WeightSum(lambda d, yy: dot_tn(own_h[d * 2 + yy], gu[...]), "ww", s.grad_w, *room(4, width))
-
-    def third_phase(t):
-        @pl.when(t < NP)
-        def _():
-            agg_forward(t)
-            agg_finish(t)
-            make_u(t)
-
-        @pl.when((t >= 2) & (t < NP + 2))
-        def _():
-            agg_second(t - 2)
-            agg_third(t - 2)
-
-        @pl.when((t >= 1) & (t < NP + 1))
-        def _():
-            make_gu(t - 1)
-            agg_first(t - 1)
-
-    loop(NP + 2, third_phase)
+    sum_w = WeightSum(lambda d, yy, first=False: dot_tn(own_h[d * 2 + yy], gu[...]), "ww", s.grad_w, *room(4, width))
+
+    def half_phases():
+        for i in range(NP):
+            agg_forward(i)
+            if i > 0:
+                make_gu(i - 1)
+                agg_first(i - 1)
+            agg_finish(i)
+            make_u(i)
+            if i > 0:
+                agg_second(i - 1)
+                agg_third(i - 1)
+        make_gu(NP - 1)
+        agg_first(NP - 1)
+        agg_second(NP - 1)
+        agg_third(NP - 1)
+
+    half_phases()
 
     def give(n):
         src, dst = ((gu2, gu.at[own_half]), (s.emb2, s.embeddings.at[own_half]))[n]
@@ -790,9 +811,11 @@
     give(1).start()
     def pass_on(i):
         arrived(grad_agg.at[(1 - x) * NP + i], sa_rs.at[2, i])
-        agg_over_y((1 - x) * NP + i)
-
-    loop(NP, pass_on)
+        if i < NP - 1:
+            agg_over_y((1 - x) * NP + i)
+
+    for i in range(NP):
+        pass_on(i)
     loop(2 * NP, lambda i: arrived(grad_agg2.at[i], s.gy_rs.at[i]))
 
     def sent_messages(q):
@@ -852,52 +875,50 @@
             for i in range(NQ)
         )
 
-    def along(j):
+    def along(j, q):
         d = dest(j)
         step = 1 - 2 * upper
         if j == 2:
             step = step * (1 - 2 * inner)
         is_dest = (0, inner, 1)[j]
         slot = d + is_dest * ((1 - step) // 2) * (4 - d)
-
-        def along_z(q):
-            own = spread(d, q)
-
-            @pl.when(inner == 0)
-            def _():
-                zsend[d, q] = own.astype(BF)
-
-            @pl.when(inner == 1)
-            def _():
-                arrived(zrecv.at[d, q], m_zr.at[d, q])
-                zsend[d, q] = (own + zrecv[d, q].astype(F32)).astype(BF)
-
-            rdma(
-                zsend.at[d, q], zrecv.at[slot, q], m_zs.at[d, q], m_zr.at[slot, q], ((z + step) * 2 + y, c)
-            ).start()
-
-        loop(NQ, along_z)
-
-    along(0)
+        own = spread(d, q)
+
+        @pl.when(inner == 0)
+        def _():
+            zsend[d, q] = own.astype(BF)
+
+        @pl.when(inner == 1)
+        def _():
+            arrived(zrecv.at[d, q], m_zr.at[d, q])
+            zsend[d, q] = (own + zrecv[d, q].astype(F32)).astype(BF)
+
+        rdma(
+            zsend.at[d, q], zrecv.at[slot, q], m_zs.at[d, q], m_zr.at[slot, q], ((z + step) * 2 + y, c)
+        ).start()
+
+    loop(NQ, lambda q: along(0, q))
 
     @pl.when(inner == 0)
     def _():
-        along(1)
-        along(2)
-
-    for n in range(2):
-        give_back(n).wait_recv()
-    store(0, 0, s.embeddings, s.embeddings_out).start()
+        for j in (1, 2):
+            loop(NQ, lambda q, j=j: along(j, q))
+
+    give_back(0).wait_recv()
     rest_forward()
     rest_finish()
     sum_w.first()
 
     @pl.when(inner == 1)
     def _():
-        along(1)
-        along(2)
-
-    sum_w.second()
+        def both_ways(q):
+            along(2, q)
+            along(1, q)
+
+        loop(NQ, both_ways)
+
+    give_back(1).wait_recv()
+    store(0, 0, s.embeddings, s.embeddings_out).start()
 
     total_t = s.total_t
 
@@ -928,16 +949,25 @@
 
     scatter_h, scatter_b = Scatter(h_part, "sh"), Scatter(b_part, "sb")
 
-    def q_part(d, yy):
-        return dot_tn(own_h[d, :, pl.ds(pl.multiple_of(yy * 128, 128), 128)], gv[...])
+
+    def q_part(d, yy, first=False):
+        n = width // 2
+        keep = u_pre.at[0, pl.ds(d * n, n)]
+        if not first:
+            return keep[...]
+        both = dot_tn(own_h[d], gv[...])
+        keep[...] = jnp.where(y == 0, both[:n], both[n:])
+        return jnp.where(y == 0, both[n:], both[:n])
 
     sum_q = WeightSum(q_part, "wq", s.grad_q, *room_narrow(6, width // 2))
     sum_p = DirectSum(s.grad_p)
     small, small_ss, small_rs = s.small, s.small_ss, s.small_rs
 
+    def column_sums(i, ref):
+        small[r, i : i + 1] = jnp.sum(ref[...].astype(F32), axis=0, keepdims=True)
+
     def send_small():
-        for i, ref in enumerate((gb, gv, gu)):
-            small[r, i : i + 1] = jnp.sum(ref[...].astype(F32), axis=0, keepdims=True)
+        column_sums(0, gb)
         for d in range(1, 8):
             rdma(
                 small.at[r], small.at[r], small_ss.at[d - 1], small_rs.at[r], ((r + d) % 8, c)
@@ -952,6 +982,15 @@
         def _():
             make_gv(t)
             scatter_h.first(t)
+
+        @pl.when((t >= 3) & (t < NQ + 2))
+        def _():
+            scatter_b.second(t - 3)
+
+        @pl.when(t == NQ - 1)
+        def _():
+            scatter_h.second(t)
+            sum_q.first()
 
         @pl.when((t >= 2) & (t < NQ + 2))
         def _():
@@ -968,34 +1007,28 @@
             scatter_b.first(q)
             store(1, q, s.grad_pin.at[at(q)], s.grad_pin_out.at[at(q)]).start()
 
-        @pl.when(t < NQ)
+        @pl.when(t < NQ - 1)
         def _():
             scatter_h.second(t)
 
-        @pl.when(t == NQ - 1)
-        def _():
-            sum_q.first()
-
-        @pl.when(t == NQ + 1)
-        def _():
-            send_small()
-
-        @pl.when((t >= 2) & (t < NQ + 2))
-        def _():
-            scatter_b.second(t - 2)
-
-        @pl.when(t == NQ + 1)
-        def _():
-            sum_q.second()
-
-        @pl.when(t >= NQ)
-        def _():
-            finish_board(t - NQ)
+        @pl.when(t == 1)
+        def _():
+            sum_w.second()
+
+        @pl.when(t == NQ)
+        def _():
+            column_sums(1, gv)
+            column_sums(2, gu)
 
     loop(NQ + 2, fourth_phase)
+    scatter_b.second(NQ - 1)
+    send_small()
+    sum_q.second()
+    for q in range(NQ - 1):
+        finish_board(q)
     sum_w.third()
     store(0, 1, s.grad_w, s.grad_w_out).start()
-    loop(NQ - 2, lambda t: finish_board(t + 2))
+    finish_board(NQ - 1)
     sum_q.third()
     store(0, 2, s.grad_q, s.grad_q_out).start()
     for d in range(1, 8):

time: 160 us -> 152 us (0.950)
  Pallas kernels: 159 us -> 151 us
    pallas_call x1, Pallas kernels: 154 us -> 147 us  [fused_device(): pl.pallas_call(functools.partial(fused_kernel, names=tuple(names)), out_s...]
where the time goes in v3:
time: 152 us
  Pallas kernels  151 us (99%)
    pallas_call x1, Pallas kernels, fused_device(): pl.pallas_call(functools.partial(fused_kernel, names=tuple(names)), out_s...  147 us
    pallas_call x1, Pallas kernels, fused_device(): pl.pallas_call(finish_kernel, out_shape=list(outs.values())[:6] + [row, r...  4.06 us

profile of v3, /device:TPU:0, one launch (start us, length us, event | category | flops | bytes accessed | tf_op | source)
XLA Modules:
  0.0 152.1 jit_solution(15915044579294562546)
XLA Ops:
  0.6 147.2 %shard_map.212 = (bf16[1024,256]{1,0:T(8,128)(2,1)}, f32[1024,256]{1,0:T(8,128)}, f32[1024,128]{1,0:T(8,128)}, f32[64,256]{1,0:T(8,128)}, f32[128,256]{1,0:T(8,1...) custom-call(bf16[1024,128]{1,0:T(8,128)(2,1)} %refs_0_.1, s32[8,128]{1,0:T(8,128)} %bitcast.15, bf16[512,256]{1,0:T(8,128)(2,1)} %refs_2_.1, ...), custom_call_target="tpu_custom_call" | custom-call | flops 15032385536 | bytes 8388608 | tf_op jit(solution)/shard_map/pallas_call | solution.py:1234
  147.9 4.1 %shard_map.213 = (bf16[1024,256]{1,0:T(8,128)(2,1)}, f32[1024,256]{1,0:T(8,128)}, f32[1024,128]{1,0:T(8,128)}, f32[64,256]{1,0:T(8,128)}, f32[128,256]{1,0:T(8,1...) custom-call(bf16[1024,256]{1,0:T(8,128)(2,1)} %get-tuple-element.29., ...), custom_call_target="tpu_custom_call" | custom-call | bytes 5242880 | tf_op jit(solution)/shard_map/pallas_call | solution.py:1246

commit v4 on v3

--- a/solution.py
+++ b/solution.py
@@ -158,13 +158,14 @@
             self.yrecv, self.zrecv = getattr(s, name + "_yrecv"), getattr(s, name + "_zrecv")
             self.ss, self.rs = getattr(s, name + "_ss"), getattr(s, name + "_rs")
 
-        def first(self):
-            def step(d):
+        def first(self, at0=0, n=4):
+            def step(i):
+                d = at0 + i
                 ref = self.ysend(d)
                 ref[...] = self.part(d, 1 - y, True).astype(BF)
                 rdma(ref, self.yrecv.at[d], self.ss.at[0, d], self.rs.at[0, d], yp).start()
 
-            loop(zn, step, unroll=zn)
+            loop(n, step, unroll=n)
 
         def second(self, at0=0, n=4):
             def step(i):
@@ -205,6 +206,45 @@
                     sent(self.zsend(d), self.ss.at[1, d])
 
             loop(zn, step)
+
+    class PairSum(WeightSum):
+        def first(self):
+            for d in ((zx + 2) % 4, zx, (z + 2) % 4, z):
+                ref = self.ysend(d)
+                ref[...] = self.part(d, 1 - y, True).astype(BF)
+                rdma(ref, self.yrecv.at[d], self.ss.at[0, d], self.rs.at[0, d], yp).start()
+
+        def total(self, d):
+            own = self.part(d, y)
+            arrived(self.yrecv.at[d], self.rs.at[0, d])
+            return own + self.yrecv[d].astype(F32)
+
+        def second(self):
+            for n, d in enumerate(((zx + 2) % 4, zx)):
+                ref = self.zsend(n)
+                ref[...] = self.total(d).astype(BF)
+                rdma(ref, self.zrecv.at[n], self.ss.at[1, n], self.rs.at[1, n], zxp).start()
+
+        def across(self):
+            d = (z + 2) % 4
+            ref = self.zsend(2)
+            own = self.total(d)
+            arrived(self.zrecv.at[0], self.rs.at[1, 0])
+            ref[...] = (own + self.zrecv[0].astype(F32)).astype(BF)
+            rdma(ref, self.zrecv.at[2], self.ss.at[1, 2], self.rs.at[1, 2], (d * 2 + y, c)).start()
+
+        def third(self):
+            own = self.total(z)
+            for n in (1, 2):
+                arrived(self.zrecv.at[n], self.rs.at[1, n])
+                own = own + self.zrecv[n].astype(F32)
+            self.out[...] = own
+
+        def drain(self):
+            for d in range(zn):
+                sent(self.ysend(d), self.ss.at[0, d])
+            for n in range(3):
+                sent(self.zsend(n), self.ss.at[1, n])
 
     class DirectSum:
         def __init__(self, out):
@@ -754,14 +794,20 @@
             sa_send[n, i] = agg_part(xs * 2 + 1 - k, i).astype(BF)
             rdma(sa_send.at[n, i], sa_recv.at[n, i], sa_ss.at[n, i], sa_rs.at[n, i], core).start()
 
+    def part_c(h):
+        return pl.ds(h * (width // 2), width // 2)
+
     def agg_second(i):
         own = agg_part(other_x, i)
         arrived(sa_recv.at[0, i], sa_rs.at[0, i])
         sa_x[i] = (own + sa_recv[0, i].astype(F32)).T.astype(BF)
-        if i == NP - 1:
-            to, there = grad_agg2.at[x * NP + i], (1 - x) * NP + i
-            rdma(sa_x.at[i], to, s.gy_ss.at[there], s.gy_rs.at[x * NP + i], diagonal).start()
-        rdma(sa_x.at[i], grad_agg.at[x * NP + i], sa_ss.at[2, i], sa_rs.at[2, i], xp).start()
+        here, there = x * NP + i, (1 - x) * NP + i
+        for h in range(2):
+            src = sa_x.at[i, part_c(h)]
+            if i == NP - 1:
+                to = grad_agg2.at[here, part_c(h)]
+                rdma(src, to, s.gy_ss.at[h, there], s.gy_rs.at[h, here], diagonal).start()
+            rdma(src, grad_agg.at[here, part_c(h)], sa_ss.at[2 + h, i], sa_rs.at[2 + h, i], xp).start()
 
     def agg_third(i):
         own = agg_part(c, i)
@@ -769,8 +815,15 @@
         grad_agg[x * NP + i] = (own + sa_recv[1, i].astype(F32)).T.astype(BF)
         agg_over_y(x * NP + i)
 
-    def agg_over_y(i):
-        rdma(grad_agg.at[i], grad_agg2.at[i], s.gy_ss.at[i], s.gy_rs.at[i], yp).start()
+    def agg_over_y(i, halves=(0, 1)):
+        for h in halves:
+            rdma(
+                grad_agg.at[i, part_c(h)],
+                grad_agg2.at[i, part_c(h)],
+                s.gy_ss.at[h, i],
+                s.gy_rs.at[h, i],
+                yp,
+            ).start()
 
     def room(at_block, n):
         return [lambda d, b=b, n=n: message.at[b, d, pl.ds(0, n)] for b in (at_block, at_block + 1)]
@@ -809,14 +862,18 @@
     give(0).start()
     rest_start()
     give(1).start()
-    def pass_on(i):
-        arrived(grad_agg.at[(1 - x) * NP + i], sa_rs.at[2, i])
-        if i < NP - 1:
-            agg_over_y((1 - x) * NP + i)
-
-    for i in range(NP):
-        pass_on(i)
-    loop(2 * NP, lambda i: arrived(grad_agg2.at[i], s.gy_rs.at[i]))
+    def arrived_x(i, h):
+        arrived(grad_agg.at[(1 - x) * NP + i, part_c(h)], sa_rs.at[2 + h, i])
+
+    for i in range(NP - 1):
+        for h in range(2):
+            arrived_x(i, h)
+            agg_over_y((1 - x) * NP + i, (h,))
+
+    def gradients_here(h):
+        arrived_x(NP - 1, h)
+        for i in range(2 * NP):
+            arrived(grad_agg2.at[i, part_c(h)], s.gy_rs.at[h, i])
 
     def sent_messages(q):
         @pl.when(z < 3)
@@ -863,25 +920,51 @@
             total = term if total is None else total + term
         return total
 
-    def spread(d, q):
+    def spread(d, q, c0=0, nc=width):
         own, other = (d * 2 + y) * NQ + q, d * NQ + q
-
-        def grads(ref, i):
-            return jnp.concatenate([ref[m] for m in range(i * each, (i + 1) * each)], axis=1)
-
+        n = sub
         return sum_of(
-            dot(grads(ref, i), tab[b, at(i)])
+            dot(ref[m, c0 : c0 + nc], tab[b, m * n : (m + 1) * n])
             for ref, tab, b in ((grad_agg, table, own), (grad_agg2, table2, other))
-            for i in range(NQ)
+            for m in range(2 * NP)
         )
 
-    def along(j, q):
+    small = s.small
+
+    def column_sums(i, ref):
+        small[r, i : i + 1] = dot(jnp.ones((16, rows), BF), ref[...])[0:1]
+
+    m_hs, m_hr = s.m_hs, s.m_hr
+
+    def target(j):
         d = dest(j)
         step = 1 - 2 * upper
         if j == 2:
             step = step * (1 - 2 * inner)
         is_dest = (0, inner, 1)[j]
         slot = d + is_dest * ((1 - step) // 2) * (4 - d)
+        return d, slot, ((z + step) * 2 + y, c)
+
+    def along_half(q, h):
+        d, slot, dev = target(0)
+        lines = part_c(h)
+        own = spread(d, q, h * (width // 2), width // 2)
+
+        @pl.when(inner == 0)
+        def _():
+            zsend[d, q, lines] = own.astype(BF)
+
+        @pl.when(inner == 1)
+        def _():
+            arrived(zrecv.at[d, q, lines], m_hr.at[d, h, q])
+            zsend[d, q, lines] = (own + zrecv[d, q, lines].astype(F32)).astype(BF)
+
+        rdma(
+            zsend.at[d, q, lines], zrecv.at[slot, q, lines], m_hs.at[h, q], m_hr.at[slot, h, q], dev
+        ).start()
+
+    def along(j, q):
+        d, slot, dev = target(j)
         own = spread(d, q)
 
         @pl.when(inner == 0)
@@ -890,24 +973,36 @@
 
         @pl.when(inner == 1)
         def _():
-            arrived(zrecv.at[d, q], m_zr.at[d, q])
+            if j == 1:
+                arrived(zrecv.at[d, q], m_zr.at[d, q])
+            else:
+                for h in range(2):
+                    arrived(zrecv.at[d, q, part_c(h)], m_hr.at[d, h, q])
             zsend[d, q] = (own + zrecv[d, q].astype(F32)).astype(BF)
 
-        rdma(
-            zsend.at[d, q], zrecv.at[slot, q], m_zs.at[d, q], m_zr.at[slot, q], ((z + step) * 2 + y, c)
-        ).start()
-
-    loop(NQ, lambda q: along(0, q))
+        rdma(zsend.at[d, q], zrecv.at[slot, q], m_zs.at[d, q], m_zr.at[slot, q], dev).start()
+
+    for h in range(2):
+        gradients_here(h)
+        loop(NQ, lambda q, h=h: along_half(q, h))
+        if h == 0:
+
+            @pl.when(inner == 1)
+            def _():
+                give_back(0).wait_recv()
+                sum_w.first(0, 2)
 
     @pl.when(inner == 0)
     def _():
         for j in (1, 2):
             loop(NQ, lambda q, j=j: along(j, q))
-
-    give_back(0).wait_recv()
+        give_back(0).wait_recv()
+        sum_w.first(0, 2)
+
     rest_forward()
     rest_finish()
-    sum_w.first()
+    sum_w.first(2, 2)
+    column_sums(2, gu)
 
     @pl.when(inner == 1)
     def _():
@@ -959,12 +1054,28 @@
         keep[...] = jnp.where(y == 0, both[:n], both[n:])
         return jnp.where(y == 0, both[n:], both[:n])
 
-    sum_q = WeightSum(q_part, "wq", s.grad_q, *room_narrow(6, width // 2))
+    sum_q = PairSum(q_part, "wq", s.grad_q, *room_narrow(6, width // 2))
     sum_p = DirectSum(s.grad_p)
-    small, small_ss, small_rs = s.small, s.small_ss, s.small_rs
-
-    def column_sums(i, ref):
-        small[r, i : i + 1] = jnp.sum(ref[...].astype(F32), axis=0, keepdims=True)
+    small_ss, small_rs = s.small_ss, s.small_rs
+
+    def so_far(d):
+        return u_pre.at[1, pl.ds(d * bwidth, bwidth)]
+
+    def add_proj(q):
+        for d in range(4):
+            got = dot_tn(boards[d, at(q)], gb[at(q)])
+
+            @pl.when(q == 0)
+            def _():
+                so_far(d)[...] = got
+
+            @pl.when(q > 0)
+            def _():
+                so_far(d)[...] += got
+
+    def proj_part(d):
+        last = slice((NQ - 1) * chunk, NQ * chunk)
+        return so_far(d)[...] + dot_tn(boards[d, last], gb[last])
 
     def send_small():
         column_sums(0, gb)
@@ -1002,7 +1113,7 @@
 
             @pl.when(t == NQ + 1)
             def _():
-                sum_p.first(lambda d: dot_tn(boards[d], gb[...]))
+                sum_p.first(proj_part)
 
             scatter_b.first(q)
             store(1, q, s.grad_pin.at[at(q)], s.grad_pin_out.at[at(q)]).start()
@@ -1011,21 +1122,20 @@
         def _():
             scatter_h.second(t)
 
-        @pl.when(t == 1)
-        def _():
-            sum_w.second()
-
-        @pl.when(t == NQ)
-        def _():
-            column_sums(1, gv)
-            column_sums(2, gu)
-
+
+        @pl.when((t >= 2) & (t <= NQ))
+        def _():
+            add_proj(t - 2)
+
+    sum_w.second()
     loop(NQ + 2, fourth_phase)
+    sum_q.second()
     scatter_b.second(NQ - 1)
+    column_sums(1, gv)
     send_small()
-    sum_q.second()
     for q in range(NQ - 1):
         finish_board(q)
+    sum_q.across()
     sum_w.third()
     store(0, 1, s.grad_w, s.grad_w_out).start()
     finish_board(NQ - 1)
@@ -1055,7 +1165,7 @@
         store(1, q, s.grad_pin.at[at(q)], s.grad_pin_out.at[at(q)]).wait()
         store(2, q, s.grad_board.at[at(q)], s.grad_board_out.at[at(q)]).wait()
         for d in range(4):
-            @pl.when(d != z)
+            @pl.when((d != z) & (d != dest(0)))
             def _():
                 sent(zsend.at[d, q], m_zs.at[d, q])
 
@@ -1066,7 +1176,8 @@
             sent(agg_ref(c, mine(i)), ga_ss.at[n, i])
         for n in range(2):
             sent(sa_send.at[n, i], sa_ss.at[n, i])
-        sent(sa_x.at[i], sa_ss.at[2, i])
+        for h in range(2):
+            sent(sa_x.at[i, part_c(h)], sa_ss.at[2 + h, i])
         sent(stat.at[0, i], stat_ss.at[i])
 
     loop(NP, drain_half)
@@ -1076,7 +1187,9 @@
         lend(n).wait_send()
     for n in range(2):
         lend_list(n).wait_send()
-    loop(2 * NP, lambda i: sent(grad_agg.at[i], s.gy_ss.at[i]))
+    for h in range(2):
+        loop(2 * NP, lambda i, h=h: sent(grad_agg.at[i, part_c(h)], s.gy_ss.at[h, i]))
+        loop(NQ, lambda q, h=h: sent(zsend.at[dest(0), q, part_c(h)], m_hs.at[h, q]))
     for n in range(2):
         give(n).wait_send()
     sum_w.drain()
@@ -1173,8 +1286,8 @@
         sa_send=vmem((2, NP, rows // 2 // NP, width), BF),
         sa_recv=vmem((2, NP, rows // 2 // NP, width), BF),
         sa_x=vmem((NP, width, rows // 2 // NP), BF),
-        sa_ss=dma((3, NP)),
-        sa_rs=dma((3, NP)),
+        sa_ss=dma((4, NP)),
+        sa_rs=dma((4, NP)),
         ga_ss=dma((3, NP + 1)),
         ga_rs=dma((3, NP + 1)),
         lend_ss=dma((4,)),
@@ -1200,8 +1313,10 @@
         m_zr=dma((5, NQ)),
         list_ss=dma((2,)),
         list_rs=dma((2,)),
-        gy_ss=dma((2 * NP,)),
-        gy_rs=dma((2 * NP,)),
+        gy_ss=dma((2, 2 * NP)),
+        gy_rs=dma((2, 2 * NP)),
+        m_hs=dma((2, NQ)),
+        m_hr=dma((4, 2, NQ)),
         small_ss=dma((7,)),
         small_rs=dma((8,)),
     )

time: 152 us -> 150 us (0.987); the launches traced: 152 us -> 148 us
  Pallas kernels: 151 us -> 147 us
    pallas_call x1, Pallas kernels: 147 us -> 143 us  [fused_device(): pl.pallas_call(functools.partial(fused_kernel, names=tuple(names)), out_s...]
where the time goes in v4:
time: 150 us; the launch traced here: 148 us
  Pallas kernels  147 us (98%)
    pallas_call x1, Pallas kernels, fused_device(): pl.pallas_call(functools.partial(fused_kernel, names=tuple(names)), out_s...  143 us
    pallas_call x1, Pallas kernels, fused_device(): pl.pallas_call(finish_kernel, out_shape=list(outs.values())[:6] + [row, r...  4.06 us

profile of v4, /device:TPU:0, one launch (start us, length us, event | category | flops | bytes accessed | tf_op | source)
XLA Modules:
  0.0 147.9 jit_solution(5361503235794472996)
XLA Ops:
  0.6 143.0 %shard_map.212 = (bf16[1024,256]{1,0:T(8,128)(2,1)}, f32[1024,256]{1,0:T(8,128)}, f32[1024,128]{1,0:T(8,128)}, f32[64,256]{1,0:T(8,128)}, f32[128,256]{1,0:T(8,1...) custom-call(bf16[1024,128]{1,0:T(8,128)(2,1)} %refs_0_.1, s32[8,128]{1,0:T(8,128)} %bitcast.15, bf16[512,256]{1,0:T(8,128)(2,1)} %refs_2_.1, ...), custom_call_target="tpu_custom_call" | custom-call | flops 15032385536 | bytes 8388608 | tf_op jit(solution)/shard_map/pallas_call | solution.py:1349
  143.7 4.1 %shard_map.213 = (bf16[1024,256]{1,0:T(8,128)(2,1)}, f32[1024,256]{1,0:T(8,128)}, f32[1024,128]{1,0:T(8,128)}, f32[64,256]{1,0:T(8,128)}, f32[128,256]{1,0:T(8,1...) custom-call(bf16[1024,256]{1,0:T(8,128)(2,1)} %get-tuple-element.29., ...), custom_call_target="tpu_custom_call" | custom-call | bytes 5242880 | tf_op jit(solution)/shard_map/pallas_call | solution.py:1361

commit v5 on v4

--- a/solution.py
+++ b/solution.py
@@ -245,49 +245,6 @@
                 sent(self.ysend(d), self.ss.at[0, d])
             for n in range(3):
                 sent(self.zsend(n), self.ss.at[1, n])
-
-    class DirectSum:
-        def __init__(self, out):
-            self.out, self.send, self.recv = out, s.wp_send, s.wp_recv
-            self.ss, self.rs = s.wp_ss, s.wp_rs
-
-        def first(self, part):
-            n = self.out.shape[0]
-
-            def step(d):
-                both = part(d)
-                for yy in range(2):
-                    block = both[yy * n : (yy + 1) * n]
-                    row = d * 2 + yy
-
-                    @pl.when(row == r)
-                    def _():
-                        self.out[...] = block
-
-                    @pl.when(row != r)
-                    def _():
-                        ref = self.send.at[row]
-                        ref[...] = block.astype(BF)
-                        rdma(ref, self.recv.at[r], self.ss.at[row], self.rs.at[r], (row, c)).start()
-
-            loop(zn, step)
-
-        def second(self):
-            def step(row):
-                @pl.when(row != r)
-                def _():
-                    arrived(self.recv.at[row], self.rs.at[row])
-                    self.out[...] += self.recv[row].astype(F32)
-
-            loop(2 * zn, step)
-
-        def drain(self):
-            def step(row):
-                @pl.when(row != r)
-                def _():
-                    sent(self.send.at[row], self.ss.at[row])
-
-            loop(2 * zn, step)
 
     barrier = pltpu.get_barrier_semaphore()
 
@@ -1055,7 +1012,6 @@
         return jnp.where(y == 0, both[n:], both[:n])
 
     sum_q = PairSum(q_part, "wq", s.grad_q, *room_narrow(6, width // 2))
-    sum_p = DirectSum(s.grad_p)
     small_ss, small_rs = s.small_ss, s.small_rs
 
     def so_far(d):
@@ -1073,9 +1029,17 @@
             def _():
                 so_far(d)[...] += got
 
-    def proj_part(d):
+    def proj_part(d, yy, first=False):
         last = slice((NQ - 1) * chunk, NQ * chunk)
-        return so_far(d)[...] + dot_tn(boards[d, last], gb[last])
+        n = bwidth // 2
+        both = so_far(d)[...]
+        if first:
+            both = both + dot_tn(boards[d, last], gb[last])
+            so_far(d)[...] = both
+            return jnp.where(y == 0, both[n:], both[:n])
+        return jnp.where(y == 0, both[:n], both[n:])
+
+    sum_p = WeightSum(proj_part, "wp", s.grad_p, *room_narrow(7, bwidth // 2))
 
     def send_small():
         column_sums(0, gb)
@@ -1113,7 +1077,8 @@
 
             @pl.when(t == NQ + 1)
             def _():
-                sum_p.first(proj_part)
+                sum_p.first()
+                sum_q.second()
 
             scatter_b.first(q)
             store(1, q, s.grad_pin.at[at(q)], s.grad_pin_out.at[at(q)]).start()
@@ -1128,15 +1093,51 @@
             add_proj(t - 2)
 
     sum_w.second()
-    loop(NQ + 2, fourth_phase)
-    sum_q.second()
+    for t in range(NQ + 2):
+        fourth_phase(t)
     scatter_b.second(NQ - 1)
     column_sums(1, gv)
     send_small()
     for q in range(NQ - 1):
         finish_board(q)
+    def drain_early(q):
+        gather_b.drain(q)
+        gather_h.drain(q)
+        scatter_h.drain(q)
+        for d in range(4):
+
+            @pl.when((d != z) & (d != dest(0)))
+            def _():
+                sent(zsend.at[d, q], m_zs.at[d, q])
+
+    loop(NQ, drain_early)
+
+    def drain_half(i):
+        for n in range(3):
+            sent(agg_ref(c, mine(i)), ga_ss.at[n, i])
+        for n in range(2):
+            sent(sa_send.at[n, i], sa_ss.at[n, i])
+        for h in range(2):
+            sent(sa_x.at[i, part_c(h)], sa_ss.at[2 + h, i])
+        sent(stat.at[0, i], stat_ss.at[i])
+
+    loop(NP, drain_half)
+    for n in range(3):
+        sent(agg_ref(c, own_half), ga_ss.at[n, NP])
+    for n in range(4):
+        lend(n).wait_send()
+    for n in range(2):
+        lend_list(n).wait_send()
+    for h in range(2):
+        loop(2 * NP, lambda i, h=h: sent(grad_agg.at[i, part_c(h)], s.gy_ss.at[h, i]))
+        loop(NQ, lambda q, h=h: sent(zsend.at[dest(0), q, part_c(h)], m_hs.at[h, q]))
+    for n in range(2):
+        give(n).wait_send()
+
+    sum_p.second()
     sum_q.across()
     sum_w.third()
+    sum_w.drain()
     store(0, 1, s.grad_w, s.grad_w_out).start()
     finish_board(NQ - 1)
     sum_q.third()
@@ -1154,45 +1155,15 @@
     s.sums[...] = total
     s.sums[3:4] = total[3:4] * per
     store(0, 3, s.sums, s.sums_out).start()
-    sum_p.second()
+    sum_p.third()
     store(3, 0, s.grad_p, s.grad_p_out).start()
 
     def drain(q):
-        gather_b.drain(q)
-        gather_h.drain(q)
-        scatter_h.drain(q)
         scatter_b.drain(q)
         store(1, q, s.grad_pin.at[at(q)], s.grad_pin_out.at[at(q)]).wait()
         store(2, q, s.grad_board.at[at(q)], s.grad_board_out.at[at(q)]).wait()
-        for d in range(4):
-            @pl.when((d != z) & (d != dest(0)))
-            def _():
-                sent(zsend.at[d, q], m_zs.at[d, q])
 
     loop(NQ, drain)
-
-    def drain_half(i):
-        for n in range(3):
-            sent(agg_ref(c, mine(i)), ga_ss.at[n, i])
-        for n in range(2):
-            sent(sa_send.at[n, i], sa_ss.at[n, i])
-        for h in range(2):
-            sent(sa_x.at[i, part_c(h)], sa_ss.at[2 + h, i])
-        sent(stat.at[0, i], stat_ss.at[i])
-
-    loop(NP, drain_half)
-    for n in range(3):
-        sent(agg_ref(c, own_half), ga_ss.at[n, NP])
-    for n in range(4):
-        lend(n).wait_send()
-    for n in range(2):
-        lend_list(n).wait_send()
-    for h in range(2):
-        loop(2 * NP, lambda i, h=h: sent(grad_agg.at[i, part_c(h)], s.gy_ss.at[h, i]))
-        loop(NQ, lambda q, h=h: sent(zsend.at[dest(0), q, part_c(h)], m_hs.at[h, q]))
-    for n in range(2):
-        give(n).wait_send()
-    sum_w.drain()
     sum_q.drain()
     sum_p.drain()
     for d in range(7):
@@ -1334,15 +1305,11 @@
         scratch[name + "_recvx"] = vmem((NQ, chunk, w), BF)
         scratch[name + "_ss"] = dma((3, NQ))
         scratch[name + "_rs"] = dma((3, NQ))
-    for name, n in (("ww", width), ("wq", width // 2)):
+    for name, n in (("ww", width), ("wq", width // 2), ("wp", bwidth // 2)):
         for part in ("_yrecv", "_zrecv"):
             scratch[name + part] = vmem((4, n, width), BF)
         scratch[name + "_ss"] = dma((2, 4))
         scratch[name + "_rs"] = dma((2, 4))
-    for name in ("wp_send", "wp_recv"):
-        scratch[name] = vmem((8, bwidth // 2, width), BF)
-    for name in ("wp_ss", "wp_rs"):
-        scratch[name] = dma((8,))
     place = pl.BlockSpec(memory_space=pl.ANY)
     whole = pl.BlockSpec(memory_space=pltpu.VMEM)
     names = [n + "_in" for n in inputs] + [n + "_out" for n in outs] + list(scratch)

time: 150 us -> 149 us (level); the launches traced: 148 us -> 148 us
  no operation moved by 1% of the time
where the time goes in v5:
time: 149 us; the launch traced here: 148 us
  Pallas kernels  148 us (99%)
    pallas_call x1, Pallas kernels, fused_device(): pl.pallas_call(functools.partial(fused_kernel, names=tuple(names)), out_s...  144 us
    pallas_call x1, Pallas kernels, fused_device(): pl.pallas_call(finish_kernel, out_shape=list(outs.values())[:6] + [row, r...  4.06 us

profile of v5, /device:TPU:0, one launch (start us, length us, event | category | flops | bytes accessed | tf_op | source)
XLA Modules:
  0.0 148.5 jit_solution(3901501865288284810)
XLA Ops:
  0.6 143.6 %shard_map.212 = (bf16[1024,256]{1,0:T(8,128)(2,1)}, f32[1024,256]{1,0:T(8,128)}, f32[1024,128]{1,0:T(8,128)}, f32[64,256]{1,0:T(8,128)}, f32[128,256]{1,0:T(8,1...) custom-call(bf16[1024,128]{1,0:T(8,128)(2,1)} %refs_0_.1, s32[8,128]{1,0:T(8,128)} %bitcast.15, bf16[512,256]{1,0:T(8,128)(2,1)} %refs_2_.1, ...), custom_call_target="tpu_custom_call" | custom-call | flops 15032385536 | bytes 8388608 | tf_op jit(solution)/shard_map/pallas_call | solution.py:1316
  144.2 4.1 %shard_map.213 = (bf16[1024,256]{1,0:T(8,128)(2,1)}, f32[1024,256]{1,0:T(8,128)}, f32[1024,128]{1,0:T(8,128)}, f32[64,256]{1,0:T(8,128)}, f32[128,256]{1,0:T(8,1...) custom-call(bf16[1024,256]{1,0:T(8,128)(2,1)} %get-tuple-element.29., ...), custom_call_target="tpu_custom_call" | custom-call | bytes 5242880 | tf_op jit(solution)/shard_map/pallas_call | solution.py:1328

commit v6 on v5

--- a/solution.py
+++ b/solution.py
@@ -1134,11 +1134,11 @@
     for n in range(2):
         give(n).wait_send()
 
-    sum_p.second()
-    sum_q.across()
     sum_w.third()
     sum_w.drain()
     store(0, 1, s.grad_w, s.grad_w_out).start()
+    sum_p.second()
+    sum_q.across()
     finish_board(NQ - 1)
     sum_q.third()
     store(0, 2, s.grad_q, s.grad_q_out).start()

time: 149 us -> 149 us (level)
  no operation moved by 1% of the time
where the time goes in v6:
time: 149 us; the launch traced here: 148 us
  Pallas kernels  148 us (99%)
    pallas_call x1, Pallas kernels, fused_device(): pl.pallas_call(functools.partial(fused_kernel, names=tuple(names)), out_s...  144 us
    pallas_call x1, Pallas kernels, fused_device(): pl.pallas_call(finish_kernel, out_shape=list(outs.values())[:6] + [row, r...  4.06 us

profile of v6, /device:TPU:0, one launch (start us, length us, event | category | flops | bytes accessed | tf_op | source)
XLA Modules:
  0.0 148.5 jit_solution(3729316358726450140)
XLA Ops:
  0.6 143.6 %shard_map.212 = (bf16[1024,256]{1,0:T(8,128)(2,1)}, f32[1024,256]{1,0:T(8,128)}, f32[1024,128]{1,0:T(8,128)}, f32[64,256]{1,0:T(8,128)}, f32[128,256]{1,0:T(8,1...) custom-call(bf16[1024,128]{1,0:T(8,128)(2,1)} %refs_0_.1, s32[8,128]{1,0:T(8,128)} %bitcast.15, bf16[512,256]{1,0:T(8,128)(2,1)} %refs_2_.1, ...), custom_call_target="tpu_custom_call" | custom-call | flops 15032385536 | bytes 8388608 | tf_op jit(solution)/shard_map/pallas_call | solution.py:1316
  144.2 4.1 %shard_map.213 = (bf16[1024,256]{1,0:T(8,128)(2,1)}, f32[1024,256]{1,0:T(8,128)}, f32[1024,128]{1,0:T(8,128)}, f32[64,256]{1,0:T(8,128)}, f32[128,256]{1,0:T(8,1...) custom-call(bf16[1024,256]{1,0:T(8,128)(2,1)} %get-tuple-element.29., ...), custom_call_target="tpu_custom_call" | custom-call | bytes 5242880 | tf_op jit(solution)/shard_map/pallas_call | solution.py:1328
